TPU v7x, 32 devices: a whole 2x2x4 slice. The times are simulated.
32 devices in a mesh: ctx: 16 (over z, y, x), wt: 2 (over core).
Axes of the slice: x: 2, y: 2, z: 4, core: 2. Of those that a mesh axis runs over, the one named last changes fastest.
Arguments:
- tokens: bfloat16 [2, 4096, 1024], P('wt', 'ctx'), may hold values from -6 to 6
- block_table: int32 [16, 2], P('ctx'), may hold values from 0 to 31, as said below
- doc_flags: int32 [2, 4096], P('wt', 'ctx'), may hold values from 0 to 1, as said below
- w_query: float32 [1024, 1024], P(('ctx', 'wt')), may hold values from -0.1875 to 0.1875
- key_weight: float32 [1024, 512], P(('ctx', 'wt')), may hold values from -0.1875 to 0.1875
- value_weight: float32 [1024, 512], P(('ctx', 'wt')), may hold values from -0.1875 to 0.1875
- w_out: float32 [1024, 1024], P(('ctx', 'wt')), may hold values from -2 to 2
- w_gate: float32 [1024, 4608], P(('ctx', 'wt')), may hold values from -0.1875 to 0.1875
- w_up: float32 [1024, 4608], P(('ctx', 'wt')), may hold values from -0.1875 to 0.1875
- w_down: float32 [1024, 4608], P(('ctx', 'wt')), may hold values from -0.09375 to 0.09375
- gain_attn: float32 [1024], P(('ctx', 'wt')), may hold values from 0.25 to 1.75
- gain_mlp: float32 [1024], P(('ctx', 'wt')), may hold values from 0.25 to 1.75
- gain_q: float32 [64], replicated, may hold values from 0.25 to 1.75
- key_norm_gain: float32 [64], replicated, may hold values from 0.25 to 1.75
- cotangent: bfloat16 [2, 4096, 1024], P('wt', 'ctx'), may hold values from -6 to 6
Outputs:
- layer_out: bfloat16 [2, 4096, 1024], P('wt', 'ctx')
- grad_input: float32 [2, 4096, 1024], P('wt', 'ctx')
- grad_query: float32 [1024, 1024], P(('ctx', 'wt'))
- grad_key: float32 [1024, 512], P(('ctx', 'wt'))
- grad_value: float32 [1024, 512], P(('ctx', 'wt'))
- grad_wout: float32 [1024, 1024], P(('ctx', 'wt'))
- grad_gate: float32 [1024, 4608], P(('ctx', 'wt'))
- grad_up: float32 [1024, 4608], P(('ctx', 'wt'))
- grad_down: float32 [1024, 4608], P(('ctx', 'wt'))
- grad_gattn: float32 [1024], P(('ctx', 'wt'))
- grad_gmlp: float32 [1024], P(('ctx', 'wt'))
- grad_gq: float32 [64], replicated
- grad_gk: float32 [64], replicated
Inputs may be any that keep to these rules, and one draw needn't show every extreme that they name: `block_table`: row c names the two blocks held at index c of ctx: a block p under 16, then 2 * 16 - 1 - p; every block of a sequence appears once; block b covers positions b * 128 to (b + 1) * 128 - 1. `doc_flags`: rows in the same order as tokens; the token at position 0 of each sequence always begins a document.
All inputs are finite; a program needn't handle non-finite values.
Results may differ from a plain program's by a relative error of at most 0.04.
Values may be sent and summed in bfloat16 or wider, within the bound.
No kernel may reach another device: no remote copies, remote signals or barrier semaphores. Data moves between devices by JAX's collectives and lax.ppermute only.
A program may use at most 320 MiB of HBM per device.

v0:
```python
import jax
import jax.numpy as jnp
from jax import lax
from jax.sharding import PartitionSpec as P

QUERY_HEADS = 16
KEY_VALUE_HEADS = 8
HEAD_SIZE = 64


epsilon = 1e-05
negative_large = -1e30


def rms_forward(value_rows, gain_vec):
    inverse = lax.rsqrt(jnp.mean(value_rows * value_rows, axis=-1, keepdims=True) + epsilon)
    return (value_rows * inverse * gain_vec, inverse)


def rms_backward(value_rows, inverse, gain_vec, grad_in):
    scaled = grad_in * gain_vec
    gain_rows = grad_in * value_rows * inverse
    grad_values = inverse * scaled - value_rows * inverse * inverse * inverse * jnp.mean(
        scaled * value_rows, axis=-1, keepdims=True
    )
    return (grad_values, gain_rows)


def rope_tables(positions):
    half_width = HEAD_SIZE // 2
    inv_freq = jnp.power(
        jnp.float32(1000000.0), -(2.0 * jnp.arange(half_width, dtype=jnp.float32)) / HEAD_SIZE
    )
    angles = positions.astype(jnp.float32)[:, None] * inv_freq[None, :]
    cosine_table = jnp.concatenate([jnp.cos(angles), jnp.cos(angles)], axis=-1)[:, None, :]
    sine_table = jnp.concatenate([jnp.sin(angles), jnp.sin(angles)], axis=-1)[:, None, :]
    return (cosine_table, sine_table)


def apply_rotary(value_rows, cosine_table, sine_table):
    half_width = HEAD_SIZE // 2
    turned = jnp.concatenate([-value_rows[..., half_width:], value_rows[..., :half_width]], axis=-1)
    return value_rows * cosine_table + turned * sine_table


def rotary_backward(grad_in, cosine_table, sine_table):
    half_width = HEAD_SIZE // 2
    sined = grad_in * sine_table
    unturned = jnp.concatenate([sined[..., half_width:], -sined[..., :half_width]], axis=-1)
    return grad_in * cosine_table + unturned


def contract_rows(left, right):
    return lax.dot_general(
        left, right, (((0,), (0,)), ((), ())), preferred_element_type=jnp.float32
    )


def contract_cols(left, right):
    return lax.dot_general(
        left, right, (((1,), (1,)), ((), ())), preferred_element_type=jnp.float32
    )


def shards(
    tokens,
    block_table,
    doc_flags,
    w_query,
    key_weight,
    value_weight,
    w_out,
    w_gate,
    w_up,
    w_down,
    gain_attn,
    gain_mlp,
    gain_q,
    key_norm_gain,
    cotangent,
):
    hidden_in = tokens[0].astype(jnp.float32)
    token_rows = hidden_in.shape[0]
    block_rows = token_rows // 2
    query_groups = QUERY_HEADS // KEY_VALUE_HEADS
    width_q = QUERY_HEADS * HEAD_SIZE
    key_value_width = KEY_VALUE_HEADS * HEAD_SIZE
    query_group_width = query_groups * HEAD_SIZE
    score_scale = HEAD_SIZE ** (-0.5)
    full_w = (
        lax.all_gather(w_query.astype(jnp.bfloat16), ("ctx", "wt"), axis=0, tiled=True),
        lax.all_gather(key_weight.astype(jnp.bfloat16), ("ctx", "wt"), axis=0, tiled=True),
        lax.all_gather(value_weight.astype(jnp.bfloat16), ("ctx", "wt"), axis=0, tiled=True),
        lax.all_gather(w_out.astype(jnp.bfloat16), ("ctx", "wt"), axis=0, tiled=True),
        lax.all_gather(w_gate.astype(jnp.bfloat16), ("ctx", "wt"), axis=0, tiled=True),
        lax.all_gather(w_up.astype(jnp.bfloat16), ("ctx", "wt"), axis=0, tiled=True),
        lax.all_gather(w_down.astype(jnp.bfloat16), ("ctx", "wt"), axis=0, tiled=True),
        lax.all_gather(gain_attn.astype(jnp.bfloat16), ("ctx", "wt"), axis=0, tiled=True),
        lax.all_gather(gain_mlp.astype(jnp.bfloat16), ("ctx", "wt"), axis=0, tiled=True),
    )
    wq_b, wk_b, wv_b, wo_b, wg_b, wu_b, wd_b, ga_b, gm_b = full_w
    gain_a = ga_b.astype(jnp.float32)
    gain_m = gm_b.astype(jnp.float32)
    own_blocks = block_table[0]
    offsets = jnp.arange(block_rows, dtype=jnp.int32)
    positions = (own_blocks[:, None] * block_rows + offsets[None, :]).reshape(-1)
    flag_pairs = doc_flags[0].reshape(2, block_rows)
    counts = jnp.sum(flag_pairs, axis=1)
    summary = jnp.concatenate([own_blocks, counts])[None, :]
    all_summary = lax.all_gather(summary, "ctx", axis=0, tiled=True)
    all_blocks = all_summary[:, 0:2].reshape(-1)
    all_counts = all_summary[:, 2:4].reshape(-1)
    before = jnp.sum(
        jnp.where(all_blocks[None, :] < own_blocks[:, None], all_counts[None, :], 0), axis=1
    )
    doc_ids = (before[:, None] + jnp.cumsum(flag_pairs, axis=1) - 1).reshape(-1)
    normed_a, inv_a = rms_forward(hidden_in, gain_a)
    normed_ab = normed_a.astype(jnp.bfloat16)
    q_raw = jnp.dot(normed_ab, wq_b, preferred_element_type=jnp.float32)
    key_unnormed = jnp.dot(normed_ab, wk_b, preferred_element_type=jnp.float32)
    value_b = jnp.dot(normed_ab, wv_b, preferred_element_type=jnp.float32).astype(jnp.bfloat16)
    cosine_table, sine_table = rope_tables(positions)
    q_heads = q_raw.reshape(token_rows, QUERY_HEADS, HEAD_SIZE)
    key_heads_split = key_unnormed.reshape(token_rows, KEY_VALUE_HEADS, HEAD_SIZE)
    q_normed, q_inv = rms_forward(q_heads, gain_q)
    k_normed, k_inv = rms_forward(key_heads_split, key_norm_gain)
    query_b = (
        apply_rotary(q_normed, cosine_table, sine_table)
        .reshape(token_rows, width_q)
        .astype(jnp.bfloat16)
    )
    key_b = (
        apply_rotary(k_normed, cosine_table, sine_table)
        .reshape(token_rows, key_value_width)
        .astype(jnp.bfloat16)
    )
    start_state = (
        jnp.full((KEY_VALUE_HEADS, query_groups, token_rows), negative_large, jnp.float32),
        jnp.zeros((KEY_VALUE_HEADS, query_groups, token_rows), jnp.float32),
        jnp.zeros((KEY_VALUE_HEADS, token_rows, query_group_width), jnp.float32),
    )
    key_p = lax.all_gather(key_b, "ctx", axis=0, tiled=True)
    value_p = lax.all_gather(value_b, "ctx", axis=0, tiled=True)
    pos_p = lax.all_gather(positions, "ctx", axis=0, tiled=True)
    doc_p = lax.all_gather(doc_ids, "ctx", axis=0, tiled=True)
    allowed = (doc_ids[:, None] == doc_p[None, :]) & (pos_p[None, :] <= positions[:, None])

    def update(current_state):

        def single_head(inputs):
            head_idx, run_max, run_sum, run_acc = inputs
            q_part = lax.dynamic_slice_in_dim(
                query_b, head_idx * query_group_width, query_group_width, 1
            ).reshape(token_rows, query_groups, HEAD_SIZE)
            k_part = lax.dynamic_slice_in_dim(key_p, head_idx * HEAD_SIZE, HEAD_SIZE, 1)
            v_part = lax.dynamic_slice_in_dim(value_p, head_idx * HEAD_SIZE, HEAD_SIZE, 1)
            scores = (
                jnp.einsum("tgd,kd->gtk", q_part, k_part, preferred_element_type=jnp.float32)
                * score_scale
            )
            new_max = jnp.maximum(
                run_max, jnp.max(jnp.where(allowed[None], scores, negative_large), axis=-1)
            )
            prob_tile = jnp.where(allowed[None], jnp.exp(scores - new_max[..., None]), 0.0)
            factor = jnp.exp(run_max - new_max)
            new_sum = run_sum * factor + jnp.sum(prob_tile, axis=-1)
            mixed_tile = jnp.einsum(
                "gtk,kd->tgd",
                prob_tile.astype(jnp.bfloat16),
                v_part,
                preferred_element_type=jnp.float32,
            ).reshape(token_rows, query_group_width)
            factor_cols = jnp.repeat(factor.T, HEAD_SIZE, axis=1)
            return (new_max, new_sum, run_acc * factor_cols + mixed_tile)

        return lax.map(
            single_head,
            (jnp.arange(KEY_VALUE_HEADS), current_state[0], current_state[1], current_state[2]),
        )

    run_max, run_sum, run_acc = lax.cond(
        jnp.any(allowed), update, lambda current_state: current_state, start_state
    )
    sum_cols = jnp.repeat(jnp.transpose(run_sum, (0, 2, 1)), HEAD_SIZE, axis=2)
    attn_out = jnp.transpose(run_acc / sum_cols, (1, 0, 2)).reshape(token_rows, width_q)
    logsumexp_heads = run_max + jnp.log(run_sum)
    lse_rows = logsumexp_heads.reshape(QUERY_HEADS, token_rows).T
    attn_b = attn_out.astype(jnp.bfloat16)
    residual = hidden_in + jnp.dot(attn_b, wo_b, preferred_element_type=jnp.float32)
    normed_m, inv_m = rms_forward(residual, gain_m)
    normed_mb = normed_m.astype(jnp.bfloat16)
    gate_pre = jnp.dot(normed_mb, wg_b, preferred_element_type=jnp.float32)
    up_pre = jnp.dot(normed_mb, wu_b, preferred_element_type=jnp.float32)
    sigmoid_g = jax.nn.sigmoid(gate_pre)
    silu_g = gate_pre * sigmoid_g
    hidden_b = (silu_g * up_pre).astype(jnp.bfloat16)
    mlp_out = contract_cols(hidden_b, wd_b)
    layer_out = (residual + mlp_out).astype(jnp.bfloat16)[None]
    back_w = (
        lax.all_gather(w_query.astype(jnp.bfloat16), ("ctx", "wt"), axis=0, tiled=True),
        lax.all_gather(key_weight.astype(jnp.bfloat16), ("ctx", "wt"), axis=0, tiled=True),
        lax.all_gather(value_weight.astype(jnp.bfloat16), ("ctx", "wt"), axis=0, tiled=True),
        lax.all_gather(w_out.astype(jnp.bfloat16), ("ctx", "wt"), axis=0, tiled=True),
        lax.all_gather(w_gate.astype(jnp.bfloat16), ("ctx", "wt"), axis=0, tiled=True),
        lax.all_gather(w_up.astype(jnp.bfloat16), ("ctx", "wt"), axis=0, tiled=True),
        lax.all_gather(w_down.astype(jnp.bfloat16), ("ctx", "wt"), axis=0, tiled=True),
        lax.all_gather(gain_attn.astype(jnp.bfloat16), ("ctx", "wt"), axis=0, tiled=True),
        lax.all_gather(gain_mlp.astype(jnp.bfloat16), ("ctx", "wt"), axis=0, tiled=True),
    )
    wq_c, wk_c, wv_c, wo_c, wg_c, wu_c, wd_c, ga_c, gm_c = back_w
    upstream = cotangent[0]
    grad_down = contract_rows(upstream, hidden_b)
    grad_hidden = jnp.dot(upstream, wd_c, preferred_element_type=jnp.float32)
    silu_slope = sigmoid_g * (1.0 + gate_pre * (1.0 - sigmoid_g))
    grad_gpre = (grad_hidden * up_pre * silu_slope).astype(jnp.bfloat16)
    grad_upre = (grad_hidden * silu_g).astype(jnp.bfloat16)
    grad_gate = contract_rows(normed_mb, grad_gpre)
    grad_up = contract_rows(normed_mb, grad_upre)
    grad_nm = contract_cols(grad_gpre, wg_c) + contract_cols(grad_upre, wu_c)
    grad_rnorm, gm_rows = rms_backward(residual, inv_m, gain_m, grad_nm)
    grad_gm_local = jnp.sum(gm_rows, axis=0)
    grad_resid = upstream.astype(jnp.float32) + grad_rnorm
    grad_branch = grad_resid.astype(jnp.bfloat16)
    grad_wout = contract_rows(attn_b, grad_branch)
    grad_attn_b = contract_cols(grad_branch, wo_c).astype(jnp.bfloat16)
    delta_by_row = jnp.sum(
        (grad_attn_b.astype(jnp.float32) * attn_out).reshape(token_rows, QUERY_HEADS, HEAD_SIZE),
        axis=-1,
    )
    delta_per_head = delta_by_row.T.reshape(KEY_VALUE_HEADS, query_groups, token_rows)
    every_logsumexp, every_delta = (
        lax.all_gather(lse_rows.astype(jnp.bfloat16), "ctx", axis=0, tiled=True).astype(
            lse_rows.dtype
        ),
        lax.all_gather(delta_by_row.astype(jnp.bfloat16), "ctx", axis=0, tiled=True).astype(
            delta_by_row.dtype
        ),
    )
    grad_key_p = lax.all_gather(key_b, "ctx", axis=0, tiled=True)
    grad_value_p = lax.all_gather(value_b, "ctx", axis=0, tiled=True)
    pos_p = lax.all_gather(positions, "ctx", axis=0, tiled=True)
    doc_p = lax.all_gather(doc_ids, "ctx", axis=0, tiled=True)
    grad_allowed = (doc_ids[:, None] == doc_p[None, :]) & (pos_p[None, :] <= positions[:, None])

    def update(acc_now):

        def single_head(inputs):
            head_idx, lse_h, delta_h = inputs
            q_part = lax.dynamic_slice_in_dim(
                query_b, head_idx * query_group_width, query_group_width, 1
            ).reshape(token_rows, query_groups, HEAD_SIZE)
            do_part = lax.dynamic_slice_in_dim(
                grad_attn_b, head_idx * query_group_width, query_group_width, 1
            ).reshape(token_rows, query_groups, HEAD_SIZE)
            k_part = lax.dynamic_slice_in_dim(grad_key_p, head_idx * HEAD_SIZE, HEAD_SIZE, 1)
            v_part = lax.dynamic_slice_in_dim(grad_value_p, head_idx * HEAD_SIZE, HEAD_SIZE, 1)
            scores = (
                jnp.einsum("tgd,kd->gtk", q_part, k_part, preferred_element_type=jnp.float32)
                * score_scale
            )
            prob_tile = jnp.where(grad_allowed[None], jnp.exp(scores - lse_h[..., None]), 0.0)
            grad_prob = jnp.einsum(
                "tgd,kd->gtk", do_part, v_part, preferred_element_type=jnp.float32
            )
            grad_score = (prob_tile * (grad_prob - delta_h[..., None])).astype(jnp.bfloat16)
            return (
                jnp.einsum(
                    "gtk,kd->tgd", grad_score, k_part, preferred_element_type=jnp.float32
                ).reshape(token_rows, query_group_width)
                * score_scale
            )

        head_pieces_split = lax.map(
            single_head, (jnp.arange(KEY_VALUE_HEADS), logsumexp_heads, delta_per_head)
        )
        return jnp.transpose(head_pieces_split, (1, 0, 2)).reshape(token_rows, width_q)

    grad_qrot = lax.cond(
        jnp.any(grad_allowed),
        update,
        lambda acc_now: acc_now,
        jnp.zeros((token_rows, width_q), jnp.float32),
    )

    def grad_keys(running, pieces):
        q_p, do_p, pos_p, doc_p = pieces
        count_of_rows = q_p.shape[0]
        logsumexp_packed = every_logsumexp.T.reshape(KEY_VALUE_HEADS, query_groups, count_of_rows)
        delta_packed = every_delta.T.reshape(KEY_VALUE_HEADS, query_groups, count_of_rows)
        allowed = (doc_p[:, None] == doc_ids[None, :]) & (positions[None, :] <= pos_p[:, None])

        def update(current_state):

            def single_head(inputs):
                head_idx, lse_h, delta_h = inputs
                q_part = lax.dynamic_slice_in_dim(
                    q_p, head_idx * query_group_width, query_group_width, 1
                ).reshape(count_of_rows, query_groups, HEAD_SIZE)
                do_part = lax.dynamic_slice_in_dim(
                    do_p, head_idx * query_group_width, query_group_width, 1
                ).reshape(count_of_rows, query_groups, HEAD_SIZE)
                k_part = lax.dynamic_slice_in_dim(key_b, head_idx * HEAD_SIZE, HEAD_SIZE, 1)
                v_part = lax.dynamic_slice_in_dim(value_b, head_idx * HEAD_SIZE, HEAD_SIZE, 1)
                scores = (
                    jnp.einsum("tgd,kd->gtk", q_part, k_part, preferred_element_type=jnp.float32)
                    * score_scale
                )
                prob_tile = jnp.where(allowed[None], jnp.exp(scores - lse_h[..., None]), 0.0)
                grad_prob = jnp.einsum(
                    "tgd,kd->gtk", do_part, v_part, preferred_element_type=jnp.float32
                )
                grad_score = (prob_tile * (grad_prob - delta_h[..., None])).astype(jnp.bfloat16)
                key_part = (
                    jnp.einsum(
                        "gtk,tgd->kd", grad_score, q_part, preferred_element_type=jnp.float32
                    )
                    * score_scale
                )
                value_part = jnp.einsum(
                    "gtk,tgd->kd",
                    prob_tile.astype(jnp.bfloat16),
                    do_part,
                    preferred_element_type=jnp.float32,
                )
                return (key_part, value_part)

            key_pieces, value_pieces = lax.map(
                single_head, (jnp.arange(KEY_VALUE_HEADS), logsumexp_packed, delta_packed)
            )
            return (
                jnp.transpose(key_pieces, (1, 0, 2)).reshape(token_rows, key_value_width),
                jnp.transpose(value_pieces, (1, 0, 2)).reshape(token_rows, key_value_width),
            )

        return lax.cond(jnp.any(allowed), update, lambda current_state: current_state, running)

    zero_kv = jnp.zeros((token_rows, key_value_width), jnp.float32)
    grad_key_rotated, grad_vfull = grad_keys(
        (zero_kv, zero_kv),
        (
            lax.all_gather(query_b, "ctx", axis=0, tiled=True),
            lax.all_gather(grad_attn_b, "ctx", axis=0, tiled=True),
            lax.all_gather(positions, "ctx", axis=0, tiled=True),
            lax.all_gather(doc_ids, "ctx", axis=0, tiled=True),
        ),
    )
    grad_qn = rotary_backward(
        grad_qrot.reshape(token_rows, QUERY_HEADS, HEAD_SIZE), cosine_table, sine_table
    )
    grad_qraw, gq_rows = rms_backward(q_heads, q_inv, gain_q, grad_qn)
    grad_key_normed = rotary_backward(
        grad_key_rotated.reshape(token_rows, KEY_VALUE_HEADS, HEAD_SIZE), cosine_table, sine_table
    )
    grad_kraw, gk_rows = rms_backward(key_heads_split, k_inv, key_norm_gain, grad_key_normed)
    grad_gq_local = jnp.sum(gq_rows, axis=(0, 1))
    grad_gk_local = jnp.sum(gk_rows, axis=(0, 1))
    grad_qb = grad_qraw.reshape(token_rows, width_q).astype(jnp.bfloat16)
    grad_kb = grad_kraw.reshape(token_rows, key_value_width).astype(jnp.bfloat16)
    grad_vb = grad_vfull.astype(jnp.bfloat16)
    grad_query = contract_rows(normed_ab, grad_qb)
    grad_key = contract_rows(normed_ab, grad_kb)
    grad_value = contract_rows(normed_ab, grad_vb)
    grad_na = (
        contract_cols(grad_qb, wq_c) + contract_cols(grad_kb, wk_c) + contract_cols(grad_vb, wv_c)
    )
    grad_anorm, ga_rows = rms_backward(hidden_in, inv_a, gain_a, grad_na)
    grad_input = (grad_resid + grad_anorm)[None]
    grad_ga_local = jnp.sum(ga_rows, axis=0)
    summed = (
        lax.psum_scatter(grad_query, ("ctx", "wt"), scatter_dimension=0, tiled=True),
        lax.psum_scatter(grad_key, ("ctx", "wt"), scatter_dimension=0, tiled=True),
        lax.psum_scatter(grad_value, ("ctx", "wt"), scatter_dimension=0, tiled=True),
        lax.psum_scatter(grad_wout, ("ctx", "wt"), scatter_dimension=0, tiled=True),
        lax.psum_scatter(grad_gate, ("ctx", "wt"), scatter_dimension=0, tiled=True),
        lax.psum_scatter(grad_up, ("ctx", "wt"), scatter_dimension=0, tiled=True),
        lax.psum_scatter(grad_down, ("ctx", "wt"), scatter_dimension=0, tiled=True),
        lax.psum_scatter(grad_ga_local, ("ctx", "wt"), scatter_dimension=0, tiled=True),
        lax.psum_scatter(grad_gm_local, ("ctx", "wt"), scatter_dimension=0, tiled=True),
    )
    results = (
        summed[0],
        summed[1],
        summed[2],
        summed[3],
        summed[4],
        summed[5],
        summed[6],
        summed[7],
        summed[8],
    )
    grad_gq, grad_gk = lax.psum((grad_gq_local, grad_gk_local), ("ctx", "wt"))
    return (
        layer_out,
        grad_input,
        results[0],
        results[1],
        results[2],
        results[3],
        results[4],
        results[5],
        results[6],
        results[7],
        results[8],
        grad_gq,
        grad_gk,
    )


def solution(mesh):
    placed = (
        P("wt", "ctx", None),
        P("ctx", None),
        P("wt", "ctx"),
        P(("ctx", "wt"), None),
        P(("ctx", "wt"), None),
        P(("ctx", "wt"), None),
        P(("ctx", "wt"), None),
        P(("ctx", "wt"), None),
        P(("ctx", "wt"), None),
        P(("ctx", "wt"), None),
        P(("ctx", "wt")),
        P(("ctx", "wt")),
        P(),
        P(),
        P("wt", "ctx", None),
    )
    return jax.shard_map(
        shards,
        mesh=mesh,
        in_specs=placed,
        out_specs=(
            P("wt", "ctx", None),
            P("wt", "ctx", None),
            P(("ctx", "wt"), None),
            P(("ctx", "wt"), None),
            P(("ctx", "wt"), None),
            P(("ctx", "wt"), None),
            P(("ctx", "wt"), None),
            P(("ctx", "wt"), None),
            P(("ctx", "wt"), None),
            P(("ctx", "wt")),
            P(("ctx", "wt")),
            P(),
            P(),
        ),
        check_vma=False,
    )
```

profile of v0, /device:TPU:1, one launch (start us, length us, event | category | flops | bytes accessed | tf_op | source)
XLA Modules:
  0.0 2105.8 jit_solution(5524260142067749437)
XLA Ops:
  13.7 40.6 %all-reduce.6 = (bf16[1024]{0:T(1024)(128)(2,1)S(1)}, bf16[1024]{0:T(1024)(128)(2,1)S(1)}) all-reduce(bf16[1024]{0:T(1024)(128)(2,1)S(1)} %dynamic-update-slice.1, bf16[1024]{0:T(1024)(128)(2,1)S(1)} %dynamic-update-slice.2), channel_id=1, replica_groups=mesh['ctx'=16,'wt'=2] {'ctx','wt'}, use_global_device_ids=true, to_apply=%add.1 | all-reduce | flops 2048 | bytes 8192
  72.8 51.1 %all-gather.21.cloned.1.call-done = bf16[1024,512]{1,0:T(8,128)(2,1)} async-done(((bf16[32,512]{1,0:T(8,128)(2,1)}), bf16[1024,512]{1,0:T(8,128)(2,1)}) %all-gather.21.cloned.1.call-update) | async-done | bytes 1048592 | tf_op jit(solution)/shard_map/all_gather | solution.py:93
  130.7 52.0 %all-gather.19.cloned.1.call-done = bf16[1024,1024]{1,0:T(8,128)(2,1)} async-done(((bf16[32,1024]{1,0:T(8,128)(2,1)}), bf16[1024,1024]{1,0:T(8,128)(2,1)}) %all-gather.19.cloned.1.call-update) | async-done | bytes 2097168 | tf_op jit(solution)/shard_map/all_gather | solution.py:91
  203.5 30.6 %all-gather.2 = s32[16,1,256]{2,1,0:T(1,128)S(1)} all-gather(s32[1,1,256]{2,1,0:T(1,128)S(1)} %bitcast.404), channel_id=1, replica_groups=mesh['ctx'=16,'wt'=2] {'ctx'}, dimensions={0}, use_global_device_ids=true | all-gather | bytes 17408 | tf_op jit(solution)/shard_map/all_gather | solution.py:144
  234.4 28.8 %all-gather.1 = s32[16,1,256]{2,1,0:T(1,128)S(1)} all-gather(s32[1,1,256]{2,1,0:T(1,128)S(1)} %bitcast.405), channel_id=1, replica_groups=mesh['ctx'=16,'wt'=2] {'ctx'}, dimensions={0}, use_global_device_ids=true | all-gather | bytes 17408 | tf_op jit(solution)/shard_map/all_gather | solution.py:145
  270.3 76.5 %all-gather.23.cloned.1.call-done = bf16[4096,512]{1,0:T(8,128)(2,1)} async-done(((bf16[256,512]{1,0:T(8,128)(2,1)}), bf16[4096,512]{1,0:T(8,128)(2,1)}) %all-gather.23.cloned.1.call-update) | async-done | bytes 4194320 | tf_op jit(solution)/shard_map/all_gather | solution.py:143
  346.8 97.5 %conditional.3 = (f32[8,2,256]{2,1,0:T(2,128)}, f32[8,2,256]{2,1,0:T(2,128)}, f32[8,256,128]{1,2,0:T(8,128)}, f32[8,2,256]{2,1,0:T(2,128)S(1)}) conditional(s32[]{:T(128)} %convert_element_type.176, () %tuple.50, (pred[256,4096]{0,1:T(8,128)(4,1)S(1)}, bf16[4096,512]{0,1:T(8,128)(2,1)}, bf16[256,1024]{0,1:T(8,128)(2,1)}, ...), branch_computations={%region_7.8_spmd, %region_8.13_spmd} | conditional | flops 559974912 | bytes 38396368 | solution.py:181
  353.2 90.2 %while.33 = (s32[]{:T(128)}, f32[8,2,256]{2,1,0:T(2,128)}, f32[8,2,256]{2,1,0:T(2,128)}, f32[8,256,128]{1,2,0:T(8,128)}, pred[256,4096]{0,1:T(8,128)(4,1)S(1)}, ...) while((s32[]{:T(128)}, f32[8,2,256]{2,1,0:T(2,128)}, ...), condition=%wide.region_12.12_spmd, body=%wide.region_9.11_spmd.sunk | while | flops 559974912 | bytes 29974800 | solution.py:176
  453.1 38.2 %all-gather.27.cloned.1.call-done = bf16[1024,4608]{1,0:T(8,128)(2,1)} async-done(((bf16[32,4608]{1,0:T(8,128)(2,1)}), bf16[1024,4608]{1,0:T(8,128)(2,1)}) %all-gather.27.cloned.1.call-update) | async-done | bytes 9437200 | tf_op jit(solution)/shard_map/all_gather | solution.py:95
  499.2 75.7 %all-gather.29.cloned.1.call-done = bf16[1024,4608]{1,0:T(8,128)(2,1)} async-done(((bf16[32,4608]{1,0:T(8,128)(2,1)}), bf16[1024,4608]{1,0:T(8,128)(2,1)}) %all-gather.29.cloned.1.call-update) | async-done | bytes 9437200 | tf_op jit(solution)/shard_map/all_gather | solution.py:96
  582.8 75.7 %all-gather.31.cloned.1.call-done = bf16[1024,4608]{1,0:T(8,128)(2,1)} async-done(((bf16[32,4608]{1,0:T(8,128)(2,1)}), bf16[1024,4608]{1,0:T(8,128)(2,1)}) %all-gather.31.cloned.1.call-update) | async-done | bytes 9437200 | tf_op jit(solution)/shard_map/all_gather | solution.py:97
  688.1 143.6 %conditional.4 = (f32[256,16,64]{0,2,1:T(8,128)}) conditional(s32[]{:T(128)} %convert_element_type.176, () %tuple.52, (f32[16,256]{1,0:T(8,128)S(1)}, bf16[4096,512]{0,1:T(8,128)(2,1)}, pred[256,4096]{0,1:T(8,128)(4,1)S(1)}, bf16[256,1024]{0,1:T(8,128)(2,1)}, f32[8,2,256]{2,1,0:T(2,128)S(1)}, /*index=5*/bf16[4096,512]{1,0:T(8,128)(2,1)}, ...), branch_computations={%region_16.17_spmd, %region_17.20_spmd} | conditional | flops 817922048 | bytes 28751304 | solution.py:278
  695.0 136.7 %while.34 = (s32[]{:T(128)}, f32[8,256,128]{1,2,0:T(8,128)}, s32[8]{0:T(128)S(1)}, bf16[4096,512]{0,1:T(8,128)(2,1)}, pred[256,4096]{0,1:T(8,128)(4,1)S(1)}, /*i...) while((s32[]{:T(128)}, f32[8,256,128]{1,2,0:T(8,128)}, ...), condition=%wide.region_19.19_spmd, body=%wide.region_18.18_spmd.sunk | while | flops 817922048 | bytes 20329752 | solution.py:273
  845.2 33.1 %all_gather.81 = bf16[4096,16]{0,1:T(8,128)(2,1)S(1)} all-gather(bf16[256,16]{0,1:T(8,128)(2,1)S(1)} %bitcast.403), channel_id=1, replica_groups=mesh['ctx'=16,'wt'=2] {'ctx'}, dimensions={0}, use_global_device_ids=true | all-gather | bytes 139264 | tf_op jit(solution)/shard_map/all_gather | solution.py:232
  878.3 30.6 %all_gather.82 = bf16[4096,16]{0,1:T(8,128)(2,1)S(1)} all-gather(bf16[256,16]{0,1:T(8,128)(2,1)S(1)} %convert_element_type.214), channel_id=1, replica_groups=mesh['ctx'=16,'wt'=2] {'ctx'}, dimensions={0}, use_global_device_ids=true | all-gather | bytes 139264 | tf_op jit(solution)/shard_map/all_gather | solution.py:235
  913.0 201.2 %conditional.5 = (f32[256,8,64]{0,2,1:T(8,128)}, bf16[256,512]{0,1:T(8,128)(2,1)}) conditional(s32[]{:T(128)} %convert_element_type.210, () %tuple.54, (f32[16,4096]{1,0:T(8,128)S(1)}, f32[16,4096]{1,0:T(8,128)S(1)}, pred[4096,256]{0,1:T(8,128)(4,1)}, bf16[256,512]{0,1:T(8,128)(2,1)}, bf16[4096,1024]{0,1:T(8,128)(2,1)}, ...), branch_computations={%region_22.23_spmd, %region_23.26_spmd} | conditional | flops 1088438272 | bytes 38666728 | solution.py:335
  915.8 198.4 %while.35 = (s32[]{:T(128)}, f32[8,256,64]{1,2,0:T(8,128)}, bf16[8,256,64]{1,2,0:T(8,128)(2,1)}, pred[4096,256]{0,1:T(8,128)(4,1)}, s32[8]{0:T(128)S(1)}, /*inde...) while((s32[]{:T(128)}, f32[8,256,64]{1,2,0:T(8,128)}, ...), condition=%wide.region_25.25_spmd, body=%wide.region_24.24_spmd.sunk | while | flops 1088438272 | bytes 37093672 | solution.py:327
  1150.1 18.7 copy.84
  1182.4 46.5 %all-reduce.5 = (f32[1024]{0:T(1024)S(1)}, f32[1024]{0:T(1024)S(1)}, f32[64]{0:T(128)}, f32[64]{0:T(128)}) all-reduce(f32[1024]{0:T(1024)S(1)} %get-tuple-element.376, f32[1024]{0:T(1024)S(1)} %copy-done.38, f32[64]{0:T(128)S(1)} %get-tuple-element.372, ...), channel_id=10, replica_groups=mesh['ctx'=16,'wt'=2] {'ctx','wt'}, use_global_device_ids=true, to_apply=%region_36.37.clone | all-reduce | flops 2176 | bytes 17408
  1231.4 93.4 %reduce-scatter.12.cloned.1.call-done = f32[32,512]{1,0:T(8,128)} async-done(((f32[1024,512]{1,0:T(8,128)}), f32[32,512]{1,0:T(8,128)}) %reduce-scatter.12.cloned.1.call-update) | async-done | bytes 65552 | tf_op jit(solution)/shard_map/reduce_scatter | solution.py:371
  1324.7 135.3 %reduce-scatter.14.cloned.1.call-done = f32[32,512]{1,0:T(8,128)} async-done(((f32[1024,512]{1,0:T(8,128)}), f32[32,512]{1,0:T(8,128)}) %reduce-scatter.14.cloned.1.call-update) | async-done | bytes 65552 | tf_op jit(solution)/shard_map/reduce_scatter | solution.py:372
  1460.1 213.6 %reduce-scatter.18.cloned.1.call-done = f32[32,4608]{1,0:T(8,128)} async-done(((f32[1024,4608]{1,0:T(8,128)}), f32[32,4608]{1,0:T(8,128)}) %reduce-scatter.18.cloned.1.call-update) | async-done | bytes 589840 | tf_op jit(solution)/shard_map/reduce_scatter | solution.py:374
  1673.7 212.6 %reduce-scatter.20.cloned.1.call-done = f32[32,4608]{1,0:T(8,128)} async-done(((f32[1024,4608]{1,0:T(8,128)}), f32[32,4608]{1,0:T(8,128)}) %reduce-scatter.20.cloned.1.call-update) | async-done | bytes 589840 | tf_op jit(solution)/shard_map/reduce_scatter | solution.py:375
  1886.2 212.5 %reduce-scatter.22.cloned.1.call-done = f32[32,4608]{1,0:T(8,128)} async-done(((f32[1024,4608]{1,0:T(8,128)}), f32[32,4608]{1,0:T(8,128)}) %reduce-scatter.22.cloned.1.call-update) | async-done | bytes 589840
  (430 shorter events, 590.6 us)
Async XLA Ops:
  7.2 63.9 %copy-start.36 = (f32[64]{0:T(128)S(1)}, f32[64]{0:T(128)}, u32[]{:S(2)}) copy-start(f32[64]{0:T(128)} %param.40) | copy-start | bytes 772
  7.2 60.6 %all-gather.15.cloned.1.call-start = ((), (), s32[]{:S(2)}) async-start(), calls=%async_computation.7 | async-start | bytes 1081344 | tf_op jit(solution)/shard_map/all_gather | solution.py:92
  8.7 115.1 %all-gather.21.cloned.1.call-start = ((), (), s32[]{:S(2)}) async-start(), calls=%async_computation.10 | async-start | bytes 1081344 | tf_op jit(solution)/shard_map/all_gather | solution.py:93
  10.3 172.4 %all-gather.19.cloned.1.call-start = ((), (), s32[]{:S(2)}) async-start(), calls=%async_computation.9 | async-start | bytes 2162688 | tf_op jit(solution)/shard_map/all_gather | solution.py:91
  11.9 112.0 %copy-start = (bf16[1,256,1024]{2,1,0:T(8,128)(2,1)S(1)}, bf16[1,256,1024]{2,1,0:T(8,128)(2,1)}, u32[]{:S(2)}) copy-start(bf16[1,256,1024]{2,1,0:T(8,128)(2,1)} %param.27) | copy-start | bytes 1572868
  11.9 258.5 %all-gather.17.cloned.1.call-start = ((), (), s32[]{:S(2)}) async-start(), calls=%async_computation.8 | async-start | bytes 4456448 | tf_op jit(solution)/shard_map/all_gather | solution.py:142
  72.7 274.1 %all-gather.23.cloned.1.call-start = ((), (), s32[]{:S(2)}) async-start(), calls=%async_computation.11 | async-start | bytes 4456448 | tf_op jit(solution)/shard_map/all_gather | solution.py:143
  126.3 322.9 %all-gather.25.cloned.1.call-start = ((), (), s32[]{:S(2)}) async-start(), calls=%async_computation.12 | async-start | bytes 2162688 | tf_op jit(solution)/shard_map/all_gather | solution.py:94
  127.0 364.3 %all-gather.27.cloned.1.call-start = ((), (), s32[]{:S(2)}) async-start(), calls=%async_computation.13 | async-start | bytes 9732096 | tf_op jit(solution)/shard_map/all_gather | solution.py:95
  127.9 447.0 %all-gather.29.cloned.1.call-start = ((), (), s32[]{:S(2)}) async-start(), calls=%async_computation.14 | async-start | bytes 9732096 | tf_op jit(solution)/shard_map/all_gather | solution.py:96
  128.7 529.7 %all-gather.31.cloned.1.call-start = ((), (), s32[]{:S(2)}) async-start(), calls=%async_computation.15 | async-start | bytes 9732096 | tf_op jit(solution)/shard_map/all_gather | solution.py:97
  130.6 778.2 %all-gather.33.cloned.1.call-start = ((), (), s32[]{:S(2)}) async-start(), calls=%async_computation.16 | async-start | bytes 8912896 | tf_op jit(solution)/shard_map/all_gather | solution.py:341
  190.5 722.5 %all-gather.35.cloned.1.call-start = ((), (), s32[]{:S(2)}) async-start(), calls=%async_computation.17 | async-start | bytes 8912896 | tf_op jit(solution)/shard_map/all_gather | solution.py:342
  453.0 121.8 %copy-start.7 = (bf16[256,1024]{1,0:T(8,128)(2,1)}, bf16[256,1024]{1,0:T(8,128)(2,1)S(1)}, u32[]{:S(2)}) copy-start(bf16[256,1024]{1,0:T(8,128)(2,1)S(1)} %multiply_convert_fusion.3) | copy-start | bytes 1572868
  683.4 547.9 %reduce-scatter.10.cloned.1.call-start = ((), (), s32[]{:S(2)}) async-start(), calls=%async_computation.18 | async-start | bytes 4325376 | tf_op jit(solution)/shard_map/reduce_scatter | solution.py:370
  838.9 392.4 %reduce-scatter.16.cloned.1.call-start = ((), (), s32[]{:S(2)}) async-start(), calls=%async_computation.21 | async-start | bytes 4325376 | tf_op jit(solution)/shard_map/reduce_scatter | solution.py:373
  841.7 71.3 %copy-start.29 = (bf16[256,512]{1,0:T(8,128)(2,1)S(1)}, bf16[256,512]{1,0:T(8,128)(2,1)}, u32[]{:S(2)}) copy-start(bf16[256,512]{1,0:T(8,128)(2,1)} %convolution_convert_fusion.1) | copy-start | bytes 786436
  841.8 483.0 %reduce-scatter.12.cloned.1.call-start = ((), (), s32[]{:S(2)}) async-start(), calls=%async_computation.19 | async-start | bytes 2162688 | tf_op jit(solution)/shard_map/reduce_scatter | solution.py:371
  913.0 202.4 %copy-start.33 = (f32[256,8]{0,1:T(8,128)S(1)}, f32[256,8]{0,1:T(8,128)}, u32[]{:S(2)}) copy-start(f32[256,8]{0,1:T(8,128)} %copy-done.32) | copy-start | bytes 24580
  913.0 202.4 %copy-start.37 = (f32[64]{0:T(128)S(1)}, f32[64]{0:T(128)}, u32[]{:S(2)}) copy-start(f32[64]{0:T(128)} %param.40) | copy-start | bytes 772
  1119.8 340.3 %reduce-scatter.14.cloned.1.call-start = ((), (), s32[]{:S(2)}) async-start(), calls=%async_computation.20 | async-start | bytes 2162688 | tf_op jit(solution)/shard_map/reduce_scatter | solution.py:372
  1122.7 551.0 %reduce-scatter.18.cloned.1.call-start = ((), (), s32[]{:S(2)}) async-start(), calls=%async_computation.22 | async-start | bytes 19464192 | tf_op jit(solution)/shard_map/reduce_scatter | solution.py:374
  1130.8 755.4 %reduce-scatter.20.cloned.1.call-start = ((), (), s32[]{:S(2)}) async-start(), calls=%async_computation.23 | async-start | bytes 19464192 | tf_op jit(solution)/shard_map/reduce_scatter | solution.py:375
  1140.5 958.3 %reduce-scatter.22.cloned.1.call-start = ((), (), s32[]{:S(2)}) async-start(), calls=%async_computation.24 | async-start | bytes 19464192
  (36 other events, 451.2 us)
Sparse Core Ops, SparseCore 0:
  11.5 56.2 all-gather.14
  71.2 52.5 all-gather.20
  127.3 55.3 all-gather.18
  185.2 85.0 all-gather.16
  273.0 73.8 all-gather.22
  350.1 56.6 all-gather.24
  410.3 81.0 all-gather.26
  494.2 80.6 all-gather.28
  577.8 80.6 all-gather.30
  661.6 133.5 all-gather.32
  798.5 114.4 all-gather.34
  915.7 133.7 reduce-scatter.9
  1052.4 136.7 reduce-scatter.15
  1191.9 132.8 reduce-scatter.11
  1327.5 132.5 reduce-scatter.13
  1466.9 206.7 reduce-scatter.17
  1680.5 205.6 reduce-scatter.19
  1893.1 205.6 reduce-scatter.21
where the time goes:
time: 2120 us; the launch traced here: 2110 us
  waiting for transfers between devices  1260 us (59%)
  matrix products  389 us (18%)
  blocking collectives  221 us (10%)
  local copies, waits for them, and re-layouts  135 us (6%)
  other arithmetic  53.1 us (3%)
  loops' own time  32.9 us (2%)
    reduce_scatter x1, waiting for transfers between devices, shards(): lax.psum_scatter(grad_gate, ('ctx', 'wt'), scatter_dimension=0, tiled=True)  214 us
    unnamed x19, waiting for transfers between devices  213 us
    reduce_scatter x1, waiting for transfers between devices, shards(): lax.psum_scatter(grad_up, ('ctx', 'wt'), scatter_dimension=0, tiled=True)  213 us
    reduce_scatter x1, waiting for transfers between devices, shards(): lax.psum_scatter(grad_value, ('ctx', 'wt'), scatter_dimension=0, tiled=True)  135 us
    dot_general x24, matrix products, single_head(): jnp.einsum('tgd,kd->gtk', q_part, k_part, preferred_element_type=jnp.floa...  118 us
    unnamed x3, blocking collectives  97.8 us
    reduce_scatter x1, waiting for transfers between devices, shards(): lax.psum_scatter(grad_key, ('ctx', 'wt'), scatter_dimension=0, tiled=True)  93.4 us
    all_gather x1, waiting for transfers between devices, shards(): value_p = lax.all_gather(value_b, 'ctx', axis=0, tiled=True)  76.5 us
  transfers between devices with their start and end apart: 18, of which 14 were waited for; matrix products, arithmetic and copies ran while one was open for 27% of the time, Pallas kernels for 0%

commit v1 on v0

v1 whole, which is shorter than its diff:
```python
import functools

import jax
import jax.numpy as jnp
import numpy as np
from jax import lax
from jax.experimental import pallas as pl
from jax.experimental.pallas import tpu as pltpu
from jax.sharding import PartitionSpec as P

HEADS = 16
KV_HEADS = 8
HEAD = 64
LANES = 2 * HEAD
BLOCK = 128
EPS = 1e-05
SCALE = HEAD**-0.5
BF = jnp.bfloat16
F32 = jnp.float32
I32 = jnp.int32
QT = 512
KT = 512
VMEM_BYTES = 56 * 1024 * 1024

NN = (((1,), (0,)), ((), ()))
NT = (((1,), (1,)), ((), ()))
TN = (((0,), (0,)), ((), ()))


def dot(a, b, dims=NN):
    return lax.dot_general(a, b, dims, preferred_element_type=F32)


def params(**kw):
    return pltpu.CompilerParams(vmem_limit_bytes=VMEM_BYTES, **kw)


def in_vmem():
    return pl.BlockSpec(memory_space=pltpu.VMEM)


def in_smem():
    return pl.BlockSpec(memory_space=pltpu.SMEM)


def low_lanes(shape):
    return lax.broadcasted_iota(I32, shape, 1) < HEAD


def half_sums(value, low):
    total = jnp.sum(value, axis=-1, keepdims=True)
    first = jnp.sum(jnp.where(low, value, 0.0), axis=-1, keepdims=True)
    return jnp.where(low, first, total - first)


def half_turn(value):
    lane = lax.broadcasted_iota(I32, value.shape, 1)
    first = (lane % HEAD) < HEAD // 2
    return jnp.where(
        first,
        pltpu.roll(value, LANES - HEAD // 2, 1),
        pltpu.roll(value, HEAD // 2, 1),
    )


def project_kernel(core_ref, n_ref, w_ref, gain_ref, cos_ref, sin_ref, raw_ref, out_ref):
    rows = cos_ref.shape[0]
    is_value = core_ref[0] == 1
    raw_all = dot(n_ref[...], w_ref[...])
    raw_ref[0] = raw_all
    for s in range(2):
        raw = raw_all[s * rows : (s + 1) * rows]
        low = low_lanes(raw.shape)
        inverse = lax.rsqrt(half_sums(raw * raw, low) * (1.0 / HEAD) + EPS)
        normed = raw * inverse * gain_ref[...]
        turned = normed * cos_ref[...] + half_turn(normed) * sin_ref[...]
        kept = jnp.where(jnp.logical_or(low, jnp.logical_not(is_value)), turned, raw)
        out_ref[0, s] = kept.astype(BF)


def project(core, normed, weight, gain, cosine, sine):
    rows = cosine.shape[0]
    return pl.pallas_call(
        project_kernel,
        grid=(KV_HEADS,),
        in_specs=[
            in_smem(),
            pl.BlockSpec(normed.shape, lambda g: (0, 0)),
            pl.BlockSpec((weight.shape[0], LANES), lambda g: (0, g)),
            pl.BlockSpec((1, LANES), lambda g: (0, 0)),
            pl.BlockSpec((rows, LANES), lambda g: (0, 0)),
            pl.BlockSpec((rows, LANES), lambda g: (0, 0)),
        ],
        out_specs=[
            pl.BlockSpec((1, 2 * rows, LANES), lambda g: (g, 0, 0)),
            pl.BlockSpec((1, 2, rows, LANES), lambda g: (g, 0, 0, 0)),
        ],
        out_shape=[
            jax.ShapeDtypeStruct((KV_HEADS, 2 * rows, LANES), F32),
            jax.ShapeDtypeStruct((KV_HEADS, 2, rows, LANES), BF),
        ],
        compiler_params=params(),
        cost_estimate=pl.CostEstimate(
            flops=2 * normed.shape[0] * normed.shape[1] * weight.shape[1],
            bytes_accessed=8 << 20,
            transcendentals=0,
        ),
    )(core, normed, weight, gain, cosine, sine)


def unproject_kernel(core_ref, grad_ref, raw_ref, gain_ref, cos_ref, sin_ref, out_ref, gain_out_ref):
    rows = cos_ref.shape[0]
    is_value = core_ref[0] == 1
    for s in range(2):
        raw = raw_ref[0, s * rows : (s + 1) * rows]
        grad = grad_ref[0, s].astype(F32)
        low = low_lanes(raw.shape)
        inverse = lax.rsqrt(half_sums(raw * raw, low) * (1.0 / HEAD) + EPS)
        back = grad * cos_ref[...] + half_turn(grad * sin_ref[...])
        is_q_or_k = jnp.logical_or(low, jnp.logical_not(is_value))
        gain_rows = jnp.sum(back * raw * inverse, axis=0, keepdims=True)
        scaled = back * gain_ref[...]
        mean = half_sums(scaled * raw, low) * (1.0 / HEAD)
        moved = inverse * scaled - raw * (inverse * inverse * inverse) * mean
        out_ref[s * rows : (s + 1) * rows, :] = jnp.where(is_q_or_k, moved, grad).astype(BF)
        gain_rows = jnp.where(is_q_or_k[:1], gain_rows, 0.0)
        if s == 0:
            total = gain_rows
        else:
            total = total + gain_rows
    gain_out_ref[0] = jnp.broadcast_to(total, (8, LANES))


def unproject(core, grads, raw, gain, cosine, sine):
    rows = cosine.shape[0]
    return pl.pallas_call(
        unproject_kernel,
        grid=(KV_HEADS,),
        in_specs=[
            in_smem(),
            pl.BlockSpec((1, 2, rows, LANES), lambda g: (g, 0, 0, 0)),
            pl.BlockSpec((1, 2 * rows, LANES), lambda g: (g, 0, 0)),
            pl.BlockSpec((1, LANES), lambda g: (0, 0)),
            pl.BlockSpec((rows, LANES), lambda g: (0, 0)),
            pl.BlockSpec((rows, LANES), lambda g: (0, 0)),
        ],
        out_specs=[
            pl.BlockSpec((2 * rows, LANES), lambda g: (0, g)),
            pl.BlockSpec((1, 8, LANES), lambda g: (g, 0, 0)),
        ],
        out_shape=[
            jax.ShapeDtypeStruct((2 * rows, KV_HEADS * LANES), BF),
            jax.ShapeDtypeStruct((KV_HEADS, 8, LANES), F32),
        ],
        compiler_params=params(),
        cost_estimate=pl.CostEstimate(flops=1 << 24, bytes_accessed=8 << 20, transcendentals=0),
    )(core, grads, raw, gain, cosine, sine)


def block_rows(ref, slot):
    return ref[pl.ds(pl.multiple_of(slot * BLOCK, BLOCK), BLOCK), :]


def sum_of_parts(value):
    first = value.astype(BF)
    rest = value - first.astype(F32)
    second = rest.astype(BF)
    third = (rest - second.astype(F32)).astype(BF)
    return first, second, third


def allowed_pairs(j, pos_row, start_row):
    key_pos = j * KT + lax.broadcasted_iota(I32, (KT, 1), 0)
    return jnp.logical_and(key_pos <= pos_row, key_pos >= start_row)


def walk_keys(lims_ref, i, step, carry):
    lo, full_lo, full_hi, hi = (lims_ref[e, i] for e in range(4))
    carry = lax.fori_loop(lo, full_lo, functools.partial(step, True), carry)
    carry = lax.fori_loop(full_lo, full_hi, functools.partial(step, False), carry)
    return lax.fori_loop(full_hi, hi, functools.partial(step, True), carry)


def attend_kernel(
    core_ref, kslot_ref, qslot_ref, lims_ref, q_ref, own_ref, other_ref, pos_ref, start_ref,
    out_ref, keep_ref, lse_ref, keys, values_t, placed,
):
    q_tiles = q_ref.shape[0] // QT
    k_tiles = own_ref.shape[0] // KT
    per = KT // BLOCK
    is_first = core_ref[0] == 0
    values_t[HEAD:, :] = jnp.ones((values_t.shape[0] - HEAD, values_t.shape[1]), BF)

    def load(t, carry):
        for b in range(per):
            slot = kslot_ref[t * per + b]
            own = block_rows(own_ref, slot)[:, HEAD:]
            other = block_rows(other_ref, slot)[:, HEAD:]
            at = pl.ds(pl.multiple_of((t * per + b) * BLOCK, BLOCK), BLOCK)
            keys[at, :] = jnp.where(is_first, own, other)
            value = jnp.where(is_first, other, own).astype(F32)
            values_t[:HEAD, at] = value.T.astype(BF)
        return carry

    lax.fori_loop(0, k_tiles, load, 0)

    def tile(i, carry):
        cols = pl.ds(pl.multiple_of(i * QT, QT), QT)
        parts = [block_rows(q_ref, qslot_ref[i * (QT // BLOCK) + b])[:, :HEAD] for b in range(QT // BLOCK)]
        query_t = (jnp.concatenate(parts, axis=0).astype(F32) * SCALE).T.astype(BF)
        pos_row = pos_ref[:, cols]
        start_row = start_ref[:, cols]

        def step(masked, j, acc):
            at = pl.ds(pl.multiple_of(j * KT, KT), KT)
            p = jnp.exp(dot(keys[at, :], query_t))
            if masked:
                p = jnp.where(allowed_pairs(j, pos_row, start_row), p, 0.0)
            return acc + dot(values_t[:, at], p.astype(BF))

        acc = walk_keys(lims_ref, i, step, jnp.zeros((values_t.shape[0], QT), F32))
        total = acc[HEAD : HEAD + 1]
        mixed = acc[:HEAD] / total
        keep_ref[:, cols] = mixed
        lse_ref[:, cols] = jnp.log(total)
        rows = mixed.T
        for b in range(QT // BLOCK):
            slot = qslot_ref[i * (QT // BLOCK) + b]
            placed[pl.ds(pl.multiple_of(slot * BLOCK, BLOCK), BLOCK), :] = rows[b * BLOCK : (b + 1) * BLOCK]
        return carry

    lax.fori_loop(0, q_tiles, tile, 0)

    def pack(c, carry):
        first = placed[pl.ds(pl.multiple_of(c * 2 * BLOCK, BLOCK), BLOCK), :]
        second = placed[pl.ds(pl.multiple_of((c * 2 + 1) * BLOCK, BLOCK), BLOCK), :]
        out_ref[pl.ds(pl.multiple_of(c * BLOCK, BLOCK), BLOCK), :] = jnp.concatenate([first, second], axis=1).astype(BF)
        return carry

    lax.fori_loop(0, q_ref.shape[0] // (2 * BLOCK), pack, 0)


def attend(core, tables, queries, own, other):
    kslot, qslot, lims, pos, start = tables
    n_q, n_k = queries.shape[0], own.shape[0]
    return pl.pallas_call(
        attend_kernel,
        in_specs=[in_smem()] * 4 + [in_vmem()] * 5,
        out_specs=[in_vmem()] * 3,
        out_shape=[
            jax.ShapeDtypeStruct((n_q // 2, LANES), BF),
            jax.ShapeDtypeStruct((HEAD, n_q), F32),
            jax.ShapeDtypeStruct((1, n_q), F32),
        ],
        scratch_shapes=[
            pltpu.VMEM((n_k, HEAD), BF),
            pltpu.VMEM((HEAD + 16, n_k), BF),
            pltpu.VMEM((n_q, HEAD), F32),
        ],
        compiler_params=params(),
        cost_estimate=pl.CostEstimate(flops=8 * n_q * n_k * HEAD, bytes_accessed=8 << 20, transcendentals=n_q * n_k),
    )(core, kslot, qslot, lims, queries, own, other, pos, start)


def attend_back_kernel(
    core_ref, kslot_ref, qslot_ref, lims_ref, q_ref, own_ref, other_ref, pos_ref, start_ref,
    grad_ref, mixed_ref, lse_ref,
    dq_ref, keep_ref, send_ref,
    keys, values, keys_t, grad_keys, grad_values, grad_placed,
):
    q_tiles = q_ref.shape[0] // QT
    k_tiles = own_ref.shape[0] // KT
    per = KT // BLOCK
    is_first = core_ref[0] == 0
    ones = jnp.ones((BLOCK, HEAD), BF)

    def load(t, carry):
        for b in range(per):
            slot = kslot_ref[t * per + b]
            own = block_rows(own_ref, slot)[:, HEAD:]
            other = block_rows(other_ref, slot)[:, HEAD:]
            at = pl.ds(pl.multiple_of((t * per + b) * BLOCK, BLOCK), BLOCK)
            key = jnp.where(is_first, own, other)
            value = jnp.where(is_first, other, own)
            keys[at, :] = jnp.concatenate([key, ones], axis=1)
            values[at, :] = jnp.concatenate([value, ones], axis=1)
            keys_t[:, at] = key.astype(F32).T.astype(BF)
            grad_keys[at, :] = jnp.zeros((BLOCK, HEAD), F32)
            grad_values[at, :] = jnp.zeros((BLOCK, HEAD), F32)
        return carry

    lax.fori_loop(0, k_tiles, load, 0)

    def unpack(c, carry):
        pair = grad_ref[pl.ds(pl.multiple_of(c * BLOCK, BLOCK), BLOCK), :]
        grad_placed[pl.ds(pl.multiple_of(c * 2 * BLOCK, BLOCK), BLOCK), :] = pair[:, :HEAD]
        grad_placed[pl.ds(pl.multiple_of((c * 2 + 1) * BLOCK, BLOCK), BLOCK), :] = pair[:, HEAD:]
        return carry

    lax.fori_loop(0, q_ref.shape[0] // (2 * BLOCK), unpack, 0)

    def tile(i, carry):
        cols = pl.ds(pl.multiple_of(i * QT, QT), QT)
        slots = [qslot_ref[i * (QT // BLOCK) + b] for b in range(QT // BLOCK)]
        query_f = jnp.concatenate([block_rows(q_ref, s)[:, :HEAD] for s in slots], axis=0).astype(F32) * SCALE
        grad = jnp.concatenate([block_rows(grad_placed, s) for s in slots], axis=0)
        query = query_f.astype(BF)
        grad_t = grad.astype(F32).T
        delta = jnp.sum(grad_t * mixed_ref[:, cols], axis=0, keepdims=True)
        pad = jnp.zeros((HEAD - 3, QT), F32)
        query_t = jnp.concatenate(
            [query_f.T] + [e.astype(F32) for e in sum_of_parts(-lse_ref[:, cols])] + [pad], axis=0
        ).astype(BF)
        grad_t = jnp.concatenate([grad_t] + [e.astype(F32) for e in sum_of_parts(-delta)] + [pad], axis=0).astype(BF)
        pos_row = pos_ref[:, cols]
        start_row = start_ref[:, cols]

        def step(masked, j, acc):
            at = pl.ds(pl.multiple_of(j * KT, KT), KT)
            p = jnp.exp(dot(keys[at, :], query_t))
            if masked:
                p = jnp.where(allowed_pairs(j, pos_row, start_row), p, 0.0)
            grad_s = (p * dot(values[at, :], grad_t)).astype(BF)
            grad_values[at, :] += dot(p.astype(BF), grad)
            grad_keys[at, :] += dot(grad_s, query)
            return acc + dot(keys_t[:, at], grad_s)

        acc = walk_keys(lims_ref, i, step, jnp.zeros((HEAD, QT), F32))
        rows = (acc * SCALE).T
        rows = jnp.concatenate([rows, jnp.zeros((QT, HEAD), F32)], axis=1)
        for b in range(QT // BLOCK):
            dq_ref[pl.ds(pl.multiple_of(slots[b] * BLOCK, BLOCK), BLOCK), :] = rows[b * BLOCK : (b + 1) * BLOCK]
        return carry

    lax.fori_loop(0, q_tiles, tile, 0)

    def place(t, carry):
        zeros = jnp.zeros((BLOCK, HEAD), F32)
        for b in range(per):
            slot = kslot_ref[t * per + b]
            at = pl.ds(pl.multiple_of((t * per + b) * BLOCK, BLOCK), BLOCK)
            to = pl.ds(pl.multiple_of(slot * BLOCK, BLOCK), BLOCK)
            key, value = grad_keys[at, :], grad_values[at, :]
            mine = jnp.where(is_first, key, value)
            theirs = jnp.where(is_first, value, key)
            keep_ref[to, :] = jnp.concatenate([zeros, mine], axis=1)
            send_ref[to, :] = jnp.concatenate([zeros, theirs], axis=1).astype(BF)
        return carry

    lax.fori_loop(0, k_tiles, place, 0)


def attend_back(core, tables, queries, own, other, grads, mixed, lse):
    kslot, qslot, lims, pos, start = tables
    n_q, n_k = queries.shape[0], own.shape[0]
    return pl.pallas_call(
        attend_back_kernel,
        in_specs=[in_smem()] * 4 + [in_vmem()] * 8,
        out_specs=[in_vmem()] * 3,
        out_shape=[
            jax.ShapeDtypeStruct((n_q, LANES), F32),
            jax.ShapeDtypeStruct((n_k, LANES), F32),
            jax.ShapeDtypeStruct((n_k, LANES), BF),
        ],
        scratch_shapes=[
            pltpu.VMEM((n_k, LANES), BF),
            pltpu.VMEM((n_k, LANES), BF),
            pltpu.VMEM((HEAD, n_k), BF),
            pltpu.VMEM((n_k, HEAD), F32),
            pltpu.VMEM((n_k, HEAD), F32),
            pltpu.VMEM((n_q, HEAD), BF),
        ],
        compiler_params=params(),
        cost_estimate=pl.CostEstimate(flops=16 * n_q * n_k * HEAD, bytes_accessed=8 << 20, transcendentals=n_q * n_k),
    )(core, kslot, qslot, lims, queries, own, other, pos, start, grads, mixed, lse)


def rms(value, gain):
    inverse = lax.rsqrt(jnp.mean(value * value, axis=-1, keepdims=True) + EPS)
    return value * inverse * gain, inverse


def rms_back(value, inverse, gain, grad):
    scaled = grad * gain
    mean = jnp.mean(scaled * value, axis=-1, keepdims=True)
    moved = inverse * scaled - value * (inverse * inverse * inverse) * mean
    return moved, jnp.sum(grad * value * inverse, axis=0)


def rope_tables(positions):
    inv_freq = jnp.power(F32(1000000.0), -(2.0 * jnp.arange(HEAD // 2, dtype=F32)) / HEAD)
    angles = positions.astype(F32)[:, None] * inv_freq[None, :]
    cosine, sine = jnp.cos(angles), jnp.sin(angles)
    return (
        jnp.concatenate([cosine] * 4, axis=1),
        jnp.concatenate([-sine, sine, -sine, sine], axis=1),
    )


def make_shards(n):
    bits = n.bit_length() - 1
    order = [4, 8, 1, 2] if n == 16 else [1 << b for b in range(bits)]
    groups = n // 16
    a2a_groups = None if groups == 1 else [[t * 16 + d for d in range(16)] for t in range(groups)]
    kv_groups = None if groups == 1 else [[t * 16 + d for t in range(groups)] for d in range(16)]

    def ctx_swap(value, mask):
        return lax.ppermute(value, "ctx", [(i, i ^ mask) for i in range(n)])

    def core_swap(value):
        return lax.ppermute(value, "wt", [(0, 1), (1, 0)])

    def gather_rows(piece):
        for mask in order:
            piece = jnp.concatenate([piece, ctx_swap(piece, mask)], axis=0)
        return piece

    def scatter_rows(value):
        for level, mask in enumerate(reversed(order)):
            half = value.shape[0] // 2
            arrived = ctx_swap(value[half:], mask)
            value = value[:half].astype(F32) + arrived.astype(F32)
            if level < len(order) - 1:
                value = value.astype(BF)
        return value

    def swap_heads(value):
        return lax.all_to_all(value, "ctx", 0, 0, axis_index_groups=a2a_groups, tiled=True)

    def shards(
        tokens, block_table, doc_flags, w_query, key_weight, value_weight, w_out, w_gate, w_up, w_down,
        gain_attn, gain_mlp, gain_q, key_norm_gain, cotangent,
    ):
        width = tokens.shape[-1]
        rows = tokens.shape[1]
        owned = w_query.shape[0]
        chip_rows = 2 * owned
        me = lax.axis_index("ctx")
        core = lax.axis_index("wt")
        first = core == 0
        core_arr = core.astype(I32).reshape(1)
        slots_n = 2 * n

        def by_core(a, b, axis=0):
            return jnp.where(first, jnp.concatenate([a, b], axis=axis), jnp.concatenate([b, a], axis=axis))

        def pick(a, b):
            return jnp.where(first, a, b)

        rel = np.arange(n)
        offset = sum(((rel >> level) & 1) * mask for level, mask in enumerate(order))
        chip_of = jnp.bitwise_xor(me.astype(I32), jnp.asarray(offset, I32))
        canon = (chip_of[:, None] * chip_rows + jnp.arange(chip_rows, dtype=I32)[None, :]).reshape(-1)
        perm = (jnp.arange(width, dtype=I32)[:, None] == canon[None, :]).astype(BF)

        def chip_piece(zero, one):
            mine = pick(zero, one).astype(BF)
            theirs = pick(one, zero).astype(BF)
            return by_core(mine, core_swap(theirs))

        def halves(weight):
            half = weight.shape[1] // 2
            return chip_piece(weight[:, :half], weight[:, half:])

        q_pairs = w_query.reshape(owned, KV_HEADS, 2, HEAD)
        qk = jnp.concatenate([q_pairs[:, :, 0], key_weight.reshape(owned, KV_HEADS, HEAD)], axis=-1).reshape(owned, width)
        qv = jnp.concatenate([q_pairs[:, :, 1], value_weight.reshape(owned, KV_HEADS, HEAD)], axis=-1).reshape(owned, width)
        flag_cols = rows // owned
        own_blocks = block_table[0]
        table_col = jnp.concatenate([own_blocks.astype(F32), jnp.zeros((owned - 2,), F32)])
        extra = jnp.concatenate(
            [
                gain_attn[:, None],
                gain_mlp[:, None],
                table_col[:, None],
                doc_flags[0].reshape(owned, flag_cols).astype(F32),
                jnp.zeros((owned, LANES - 3 - flag_cols), F32),
            ],
            axis=1,
        )
        first_piece = chip_piece(jnp.concatenate([qk, extra], axis=1), jnp.concatenate([qv, extra], axis=1))
        first_full = gather_rows(first_piece)
        w_qkv = first_full[:, :width]
        extras = first_full[:, width:].astype(F32)

        x_own, c_own = tokens[0], cotangent[0]
        x_two = dot(by_core(x_own, core_swap(x_own)), perm).astype(BF)
        c_two = dot(by_core(c_own, core_swap(c_own)), perm).astype(BF)
        hidden = x_two.astype(F32)

        wo_half = gather_rows(halves(w_out))
        w_g = gather_rows(halves(w_gate))
        w_u = gather_rows(halves(w_up))
        w_d = gather_rows(halves(w_down))

        gain_a, gain_m = extras[:, 0][None, :], extras[:, 1][None, :]
        per_chip = extras.reshape(n, 2, owned, LANES)
        block_of = per_chip[:, 0, :2, 2].reshape(-1).astype(I32)
        seq = me % 2
        flags = jnp.where(seq == 0, per_chip[:, 0], per_chip[:, 1])[:, :, 3 : 3 + flag_cols].reshape(slots_n, BLOCK)
        slot_of = (chip_of[:, None] * 2 + jnp.arange(2, dtype=I32)[None, :]).reshape(-1)
        ids = jnp.arange(slots_n, dtype=I32)
        hit = ids[:, None] == block_of[None, :]
        flags_pos = dot(hit.astype(BF), flags.astype(BF))
        kslot = jnp.sum(jnp.where(hit, slot_of[None, :], 0), axis=1)
        pos = jnp.arange(slots_n * BLOCK, dtype=I32).reshape(slots_n, BLOCK)
        begins = jnp.where(flags_pos > 0.5, pos, -1)
        lane = jnp.arange(BLOCK, dtype=I32)
        inside = jnp.max(jnp.where(lane[None, None, :] <= lane[None, :, None], begins[:, None, :], -1), axis=2)
        carried = jnp.max(jnp.where(ids[None, :] < ids[:, None], jnp.max(begins, axis=1)[None, :], -1), axis=1)
        doc_start = jnp.maximum(inside, carried[:, None])
        here = (slot_of // 32) == (me // 16)
        rank = jnp.sum((here[None, :] & (block_of[None, :] < block_of[:, None])).astype(I32), axis=1)
        hit_q = here[None, :] & (rank[None, :] == jnp.arange(32, dtype=I32)[:, None])
        q_block = jnp.sum(jnp.where(hit_q, block_of[None, :], 0), axis=1)
        qslot = jnp.sum(jnp.where(hit_q, slot_of[None, :] - (me // 16) * 32, 0), axis=1)
        q_pos = q_block[:, None] * BLOCK + lane[None, :]
        q_start = jnp.sum(jnp.where((q_block[:, None] == ids[None, :])[:, :, None], doc_start[None], 0), axis=1)
        n_q = 32 * BLOCK
        tile_start = q_start.reshape(n_q // QT, QT)
        tile_pos = q_pos.reshape(n_q // QT, QT)
        low, high = jnp.min(tile_start, axis=1) // KT, jnp.max(tile_pos, axis=1) // KT + 1
        full_low = jnp.minimum((jnp.max(tile_start, axis=1) + KT - 1) // KT, high)
        full_high = jnp.maximum(jnp.minimum((jnp.min(tile_pos, axis=1) + 1) // KT, high), full_low)
        lims = jnp.stack([low, full_low, full_high, high])
        tables = (kslot, qslot, lims, q_pos.reshape(1, n_q), q_start.reshape(1, n_q))

        own_pos = (own_blocks[:, None] * BLOCK + lane[None, :]).reshape(-1)
        cosine, sine = rope_tables(own_pos)
        gain_qk = jnp.concatenate([gain_q, key_norm_gain])[None, :]

        normed_a, inv_a = rms(hidden, gain_a)
        normed_ab = normed_a.astype(BF)
        raw, packed = project(core_arr, normed_ab, w_qkv, gain_qk, cosine, sine)
        queries = swap_heads(packed.reshape(16, rows, LANES)).reshape(n_q, LANES)
        own_kv = queries
        if groups > 1:
            own_kv = lax.all_gather(queries, "ctx", axis=0, tiled=True, axis_index_groups=kv_groups)
        other_kv = core_swap(own_kv)
        mixed_packed, mixed, lse = attend(core_arr, tables, queries, own_kv, other_kv)

        def heads_to_rows(value):
            value = value.reshape(KV_HEADS, 2, BLOCK, 2, HEAD)
            return jnp.transpose(value, (1, 3, 2, 0, 4)).reshape(2 * rows, KV_HEADS * HEAD)

        def rows_to_heads(value):
            value = value.reshape(2, 2, BLOCK, KV_HEADS, HEAD)
            return jnp.transpose(value, (3, 0, 2, 1, 4)).reshape(16, BLOCK, LANES)

        wo_other = core_swap(wo_half)
        wo_full = by_core(wo_half, wo_other, axis=1)
        head_ids = jnp.arange(width, dtype=I32)
        place = (head_ids // 512).astype(I32)
        head_row = (((head_ids % 512) // HEAD) * 2 + jnp.bitwise_xor(core.astype(I32), place)) * HEAD + head_ids % HEAD
        select = (head_row[:, None] == canon[None, :]).astype(BF)
        wo_sel = dot(select, dot(wo_full, perm).astype(BF)).astype(BF)

        attn_own = heads_to_rows(swap_heads(mixed_packed.reshape(16, BLOCK, LANES)))
        attn = jnp.concatenate([attn_own, core_swap(attn_own)], axis=1)
        residual = hidden + dot(attn, wo_sel)
        normed_m, inv_m = rms(residual, gain_m)
        normed_mb = normed_m.astype(BF)

        gate = dot(normed_mb, w_g)
        up = dot(normed_mb, w_u)
        sig = jax.nn.sigmoid(gate)
        silu = gate * sig
        mid = (silu * up).astype(BF)
        grad_mid = dot(c_two, w_d)
        grad_gate_in = (grad_mid * up * (sig * (1.0 + gate * (1.0 - sig)))).astype(BF)
        grad_up_in = (grad_mid * silu).astype(BF)
        grad_n2_part = (dot(grad_gate_in, w_g, NT) + dot(grad_up_in, w_u, NT)).astype(BF)
        grad_n2 = grad_n2_part.astype(F32) + core_swap(grad_n2_part).astype(F32)
        moved_m, grad_gm = rms_back(residual, inv_m, gain_m, grad_n2)
        grad_h = c_two.astype(F32) + moved_m
        grad_hb = grad_h.astype(BF)
        grad_attn = dot(grad_hb, wo_sel[: KV_HEADS * HEAD], NT).astype(BF)
        grads_in = swap_heads(rows_to_heads(grad_attn)).reshape(n_q // 2, LANES)

        mlp_part = dot(mid, w_d, NT)
        mlp_other = core_swap(pick(mlp_part[rows:], mlp_part[:rows]))
        layer_rel = pick(residual[:rows], residual[rows:]) + (pick(mlp_part[:rows], mlp_part[rows:]) + mlp_other)
        layer_out = dot(layer_rel.astype(BF), perm, NT).astype(BF)[None]

        part_down = scatter_rows(dot(c_two, mid, TN).astype(BF))
        part_gate = scatter_rows(dot(normed_mb, grad_gate_in, TN).astype(BF))
        part_up = scatter_rows(dot(normed_mb, grad_up_in, TN).astype(BF))
        attn_rel = dot(attn, select).astype(BF)
        grad_hc = dot(grad_hb, pick(perm[: width // 2], perm[width // 2 :]), NT).astype(BF)
        part_out = scatter_rows(dot(attn_rel, grad_hc, TN).astype(BF))

        dq, keep, send = attend_back(core_arr, tables, queries, own_kv, other_kv, grads_in, mixed, lse)
        grad_kv = keep + core_swap(send).astype(F32)
        if groups > 1:
            grad_kv = lax.psum_scatter(grad_kv, "ctx", scatter_dimension=0, tiled=True, axis_index_groups=kv_groups)
        back = swap_heads((dq + grad_kv).astype(BF).reshape(16, rows, LANES))
        grad_qkv_in, gain_parts = unproject(core_arr, back.reshape(KV_HEADS, 2, rows, LANES), raw, gain_qk, cosine, sine)
        part_qkv = scatter_rows(dot(normed_ab, grad_qkv_in, TN).astype(BF))
        n1_part = dot(grad_qkv_in, w_qkv, NT)
        n1_other = core_swap(pick(n1_part[rows:], n1_part[:rows]))
        grad_n1 = pick(n1_part[:rows], n1_part[rows:]) + n1_other

        def mine(value):
            return pick(value[:rows], value[rows:])

        moved_a, grad_ga = rms_back(mine(hidden), mine(inv_a), gain_a, grad_n1)
        grad_in_rel = mine(grad_h) + moved_a
        in_hi = grad_in_rel.astype(BF)
        in_lo = (grad_in_rel - in_hi.astype(F32)).astype(BF)
        grad_input = (dot(in_hi, perm, NT) + dot(in_lo, perm, NT))[None]

        vectors = jnp.stack([grad_ga, jnp.where(first, grad_gm, 0.0)])
        vectors = lax.dot_general(
            vectors, perm.astype(F32), NT, precision=lax.Precision.HIGHEST, preferred_element_type=F32
        )
        heads_gain = jnp.sum(gain_parts[:, 0], axis=0)
        small = jnp.concatenate([vectors.reshape(-1, LANES), heads_gain[None], jnp.zeros((7, LANES), F32)])
        for mask in order:
            small = small + ctx_swap(small, mask)
        small = small + core_swap(small)
        my_row = (me * 2 + core) * owned
        gains = small[: 2 * width // LANES].reshape(2, width)
        gains = lax.dynamic_slice_in_dim(gains, my_row, owned, axis=1)

        def finish(part):
            kept = pick(part[:owned], part[owned:])
            arrived = core_swap(pick(part[owned:], part[:owned]))
            return kept, arrived

        def finish_halves(part):
            return by_core(*finish(part), axis=1)

        kept, arrived = finish(part_qkv)
        zero = pick(kept, arrived).reshape(owned, KV_HEADS, LANES)
        one = pick(arrived, kept).reshape(owned, KV_HEADS, LANES)
        grad_query = jnp.stack([zero[..., :HEAD], one[..., :HEAD]], axis=2).reshape(owned, width)
        grad_key = zero[..., HEAD:].reshape(owned, KV_HEADS * HEAD)
        grad_value = one[..., HEAD:].reshape(owned, KV_HEADS * HEAD)
        return (
            layer_out,
            grad_input,
            grad_query,
            grad_key,
            grad_value,
            finish_halves(part_out),
            finish_halves(part_gate),
            finish_halves(part_up),
            finish_halves(part_down),
            gains[0],
            gains[1],
            small[2 * width // LANES, :HEAD],
            small[2 * width // LANES, HEAD:],
        )

    return shards


def solution(mesh):
    seq = P("wt", "ctx", None)
    weight = P(("ctx", "wt"), None)
    vector = P(("ctx", "wt"))
    return jax.shard_map(
        make_shards(mesh.shape["ctx"]),
        mesh=mesh,
        in_specs=(seq, P("ctx", None), P("wt", "ctx")) + (weight,) * 7 + (vector, vector, P(), P(), seq),
        out_specs=(seq, seq) + (weight,) * 7 + (vector, vector, P(), P()),
        check_vma=False,
    )
```

time: 2120 us -> 862 us (0.41)
  waiting for transfers between devices: 1260 us -> 482 us
  matrix products: 389 us -> 74.1 us
  blocking collectives: 221 us -> 0 us
  starting transfers between devices: 0.96 us -> 103 us
  local copies, waits for them, and re-layouts: 135 us -> 61 us
  Pallas kernels: 0 us -> 63 us
  loops' own time: 32.9 us -> 0 us
    reduce_scatter x6 -> x0, waiting for transfers between devices: 655 us -> none  [the longest x1 214 us: shards(): lax.psum_scatter(grad_gate, ('ctx', 'wt'), scatter_dimension=0, tiled=True)]
    all_gather x11 -> x0, waiting for transfers between devices: 389 us -> none  [the longest x1 76.5 us: shards(): value_p = lax.all_gather(value_b, 'ctx', axis=0, tiled=True)]
    dot_general x77 -> x23, matrix products: 389 us -> 74.1 us  [the longest x22 72.2 us: dot(): return lax.dot_general(a, b, dims, preferred_element_type=F32)]
    ppermute x0 -> x64, waiting for transfers between devices: none -> 255 us  [the longest x44 255 us: ctx_swap(): return lax.ppermute(value, 'ctx', [(i, i ^ mask) for i in range(n)])]
    all_to_all x0 -> x4, waiting for transfers between devices: none -> 227 us  [swap_heads(): lax.all_to_all(value, 'ctx', 0, 0, axis_index_groups=a2a_groups, tiled=True)]
    unnamed x19 -> x0, waiting for transfers between devices: 213 us -> none
    all_gather x4 -> x0, blocking collectives: 123 us -> none  [the longest x1 33.1 us: shards(): lax.all_gather(lse_rows.astype(jnp.bfloat16), 'ctx', axis=0, tiled=True)]
    unnamed x3 -> x0, blocking collectives: 97.8 us -> none
  transfers between devices with their start and end apart: 18 -> 68, of which waited for: 14 -> 29; matrix products, arithmetic and copies ran while one was open for 27% -> 20% of each run, Pallas kernels for 0% -> 7%
where the time goes in v1:
time: 862 us; the launch traced here: 849 us
  waiting for transfers between devices  482 us (56%)
  starting transfers between devices  103 us (12%)
  matrix products  74.1 us (9%)
  other arithmetic  63 us (7%)
  Pallas kernels  63 us (7%)
  local copies, waits for them, and re-layouts  61 us (7%)
    ppermute x44, waiting for transfers between devices, ctx_swap(): return lax.ppermute(value, 'ctx', [(i, i ^ mask) for i in range(n)])  255 us
    all_to_all x4, waiting for transfers between devices, swap_heads(): lax.all_to_all(value, 'ctx', 0, 0, axis_index_groups=a2a_groups, tiled=True)  227 us
    dot_general x22, matrix products, dot(): return lax.dot_general(a, b, dims, preferred_element_type=F32)  72.2 us
    ppermute x44, starting transfers between devices, ctx_swap(): return lax.ppermute(value, 'ctx', [(i, i ^ mask) for i in range(n)])  50.3 us
    pallas_call x1, Pallas kernels, attend_back(): pl.pallas_call(attend_back_kernel, in_specs=[in_smem()] * 4 + [in_vmem()]...  27.3 us
    ppermute x20, starting transfers between devices, core_swap(): return lax.ppermute(value, 'wt', [(0, 1), (1, 0)])  26.7 us
    all_to_all x4, starting transfers between devices, swap_heads(): lax.all_to_all(value, 'ctx', 0, 0, axis_index_groups=a2a_groups, tiled=True)  26.3 us
    unnamed x145, local copies, waits for them, and re-layouts  19.6 us
  transfers between devices with their start and end apart: 68, of which 29 were waited for; matrix products, arithmetic and copies ran while one was open for 20% of the time, Pallas kernels for 7%

profile of v1, /device:TPU:1, one launch (start us, length us, event | category | flops | bytes accessed | tf_op | source)
XLA Modules:
  0.0 849.2 jit_solution(12367496366090900174)
XLA Ops:
  38.8 9.2 %collective-permute-done.20 = bf16[64,2304]{1,0:T(8,128)(2,1)S(1)} collective-permute-done((bf16[64,2304]{1,0:T(8,128)(2,1)S(1)}, bf16[64,2304]{1,0:T(8,128)(2,1)S(1)}, u32[]{:S(2)}, u32[]{:S(2)}) %collective-permute-start.20) | collective-permute-done | bytes 294944 | tf_op jit(solution)/shard_map/ppermute | solution.py:408
  74.6 32.4 %collective-permute-done.16 = bf16[128,2304]{1,0:T(8,128)(2,1)S(1)} collective-permute-done((bf16[128,2304]{1,0:T(8,128)(2,1)S(1)}, bf16[128,2304]{1,0:T(8,128)(2,1)S(1)}, u32[]{:S(2)}, u32[]{:S(2)}) %collective-permute-start.16) | collective-permute-done | bytes 589856 | tf_op jit(solution)/shard_map/ppermute | solution.py:408
  109.4 10.2 %collective-permute-done.21 = bf16[128,2304]{1,0:T(8,128)(2,1)S(1)} collective-permute-done((bf16[128,2304]{1,0:T(8,128)(2,1)S(1)}, bf16[128,2304]{1,0:T(8,128)(2,1)S(1)}, u32[]{:S(2)}, u32[]{:S(2)}) %collective-permute-start.21) | collective-permute-done | bytes 589856 | tf_op jit(solution)/shard_map/ppermute | solution.py:408
  122.1 10.2 %collective-permute-done.26 = bf16[128,2304]{1,0:T(8,128)(2,1)S(1)} collective-permute-done((bf16[128,2304]{1,0:T(8,128)(2,1)S(1)}, bf16[128,2304]{1,0:T(8,128)(2,1)S(1)}, u32[]{:S(2)}, u32[]{:S(2)}) %collective-permute-start.26) | collective-permute-done | bytes 589856 | tf_op jit(solution)/shard_map/ppermute | solution.py:408
  140.5 8.4 fusion.32
  162.1 21.0 %collective-permute-done.27 = bf16[256,2304]{1,0:T(8,128)(2,1)} collective-permute-done((bf16[256,2304]{1,0:T(8,128)(2,1)}, bf16[256,2304]{1,0:T(8,128)(2,1)}, u32[]{:S(2)}, u32[]{:S(2)}) %collective-permute-start.27) | collective-permute-done | bytes 1179680 | tf_op jit(solution)/shard_map/ppermute | solution.py:408
  202.9 9.8 %shard_map.255 = (f32[8,512,128]{2,1,0:T(8,128)}, bf16[8,2,256,128]{3,2,1,0:T(8,128)(2,1)}) custom-call(s32[1]{0:T(128)} %bitcast.1.core_ref, bf16[512,1024]{1,0:T(8,128)(2,1)} %multiply_convert_fusion.4.n_ref, bf16[1024,1024]{1,0:T(8,128)(2,1)} %slice.397.w_ref, f32[1,128]{1,0:T(1,128)} %maximum_bitcast_fusion.gain_ref, ...), custom_call_target="tpu_custom_call" | custom-call | flops 1073741824 | bytes 8388608 | tf_op jit(solution)/shard_map/pallas_call | solution.py:83
  212.7 8.9 %all-to-all-start = ((bf16[16,256,128]{2,1,0:T(8,128)(2,1)}), bf16[16,256,128]{2,1,0:T(8,128)(2,1)S(1)}, u32[]{:S(2)}, u32[]{:S(2)}) async-start(bf16[16,256,128]{2,1,0:T(8,128)(2,1)} %bitcast.186), calls=%async_computation | async-start | bytes 2097152 | tf_op jit(solution)/shard_map/all_to_all | solution.py:428
  225.2 101.8 %all-to-all-done = bf16[16,256,128]{2,1,0:T(8,128)(2,1)S(1)} async-done(((bf16[16,256,128]{2,1,0:T(8,128)(2,1)}), bf16[16,256,128]{2,1,0:T(8,128)(2,1)S(1)}, u32[]{:S(2)}, u32[]{:S(2)}) %all-to-all-start) | async-done | bytes 1048608 | tf_op jit(solution)/shard_map/all_to_all | solution.py:428
  335.7 17.5 %shard_map.256 = (bf16[2048,128]{1,0:T(8,128)(2,1)}, f32[64,4096]{1,0:T(8,128)}, f32[1,4096]{1,0:T(1,128)}) custom-call(s32[1]{0:T(128)} %bitcast.1.core_ref, s32[32]{0:T(128)} %get-tuple-element.45.kslot_ref, s32[32]{0:T(128)} %get-tuple-element.44.qslot_ref, s32[4,8]{1,0:T(4,128)} %pad_add_fusion.lims_ref, bf16[4096,128]{1,0:T(8,128)(2,1)} %bitcast.182, ...), custom_call_target="tpu_custom_call" | custom-call | flops 8589934592 | bytes 8388608 | tf_op jit(solution)/shard_map/pallas_call | solution.py:246
  355.2 8.0 all-to-all-start.1
  366.5 6.6 fusion.119
  390.9 5.9 multiply_convert_fusion.1
  452.4 12.7 %collective-permute-done.41 = bf16[128,512]{1,0:T(8,128)(2,1)S(1)} collective-permute-done((bf16[128,512]{1,0:T(8,128)(2,1)S(1)}, bf16[128,512]{1,0:T(8,128)(2,1)S(1)}, u32[]{:S(2)}, u32[]{:S(2)}) %collective-permute-start.41) | collective-permute-done | bytes 131104 | tf_op jit(solution)/shard_map/ppermute | solution.py:408
  471.6 121.9 %all-to-all-done.2 = bf16[16,128,128]{1,2,0:T(8,128)(2,1)S(1)} async-done(((bf16[16,128,128]{1,2,0:T(8,128)(2,1)}), bf16[16,128,128]{1,2,0:T(8,128)(2,1)S(1)}, u32[]{:S(2)}, u32[]{:S(2)}) %all-to-all-start.2) | async-done | bytes 524320 | tf_op jit(solution)/shard_map/all_to_all | solution.py:428
  594.5 27.3 %shard_map.257 = (f32[4096,128]{1,0:T(8,128)}, f32[4096,128]{1,0:T(8,128)}, bf16[4096,128]{1,0:T(8,128)(2,1)}) custom-call(s32[1]{0:T(128)} %bitcast.1.core_ref, s32[32]{0:T(128)} %get-tuple-element.45.kslot_ref, s32[32]{0:T(128)} %get-tuple-element.44.qslot_ref, s32[4,8]{1,0:T(4,128)} %pad_add_fusion.lims_ref, bf16[4096,128]{1,0:T(8,128)(2,1)} %bitcast.184, ...), custom_call_target="tpu_custom_call" | custom-call | flops 17179869184 | bytes 8388608 | tf_op jit(solution)/shard_map/pallas_call | solution.py:356
  645.8 11.6 %collective-permute-done.55 = bf16[256,2304]{1,0:T(8,128)(2,1)} collective-permute-done((bf16[256,2304]{1,0:T(8,128)(2,1)}, bf16[256,2304]{1,0:T(8,128)(2,1)}, u32[]{:S(2)}, u32[]{:S(2)}) %collective-permute-start.55) | collective-permute-done | bytes 1179680 | tf_op jit(solution)/shard_map/ppermute | solution.py:408
  659.9 30.5 %collective-permute-done.50 = bf16[256,2304]{1,0:T(8,128)(2,1)} collective-permute-done((bf16[256,2304]{1,0:T(8,128)(2,1)}, bf16[256,2304]{1,0:T(8,128)(2,1)}, u32[]{:S(2)}, u32[]{:S(2)}) %collective-permute-start.50) | collective-permute-done | bytes 1179680 | tf_op jit(solution)/shard_map/ppermute | solution.py:408
  693.7 22.0 %collective-permute-done.45 = bf16[256,2304]{1,0:T(8,128)(2,1)} collective-permute-done((bf16[256,2304]{1,0:T(8,128)(2,1)}, bf16[256,2304]{1,0:T(8,128)(2,1)}, u32[]{:S(2)}, u32[]{:S(2)}) %collective-permute-start.45) | collective-permute-done | bytes 1179680 | tf_op jit(solution)/shard_map/ppermute | solution.py:408
  721.8 25.1 %collective-permute-done.46 = bf16[128,2304]{1,0:T(8,128)(2,1)S(1)} collective-permute-done((bf16[128,2304]{1,0:T(8,128)(2,1)S(1)}, bf16[128,2304]{1,0:T(8,128)(2,1)S(1)}, u32[]{:S(2)}, u32[]{:S(2)}) %collective-permute-start.46) | collective-permute-done | bytes 589856 | tf_op jit(solution)/shard_map/ppermute | solution.py:408
  759.9 8.4 shard_map.258
  785.7 18.4 %collective-permute-done.34 = bf16[512,1024]{1,0:T(8,128)(2,1)} collective-permute-done((bf16[512,1024]{1,0:T(8,128)(2,1)}, bf16[512,1024]{1,0:T(8,128)(2,1)}, u32[]{:S(2)}, u32[]{:S(2)}) %collective-permute-start.34) | collective-permute-done | bytes 1048608 | tf_op jit(solution)/shard_map/ppermute | solution.py:408
  811.5 7.5 collective-permute-done.61
  826.8 11.8 %collective-permute-done.36 = bf16[128,1024]{1,0:T(8,128)(2,1)S(1)} collective-permute-done((bf16[128,1024]{1,0:T(8,128)(2,1)S(1)}, bf16[128,1024]{1,0:T(8,128)(2,1)S(1)}, u32[]{:S(2)}, u32[]{:S(2)}) %collective-permute-start.36) | collective-permute-done | bytes 262176 | tf_op jit(solution)/shard_map/ppermute | solution.py:408
  (478 shorter events, 299.4 us)
Async XLA Ops:
  9.2 51.0 %collective-permute-start = (bf16[256,1024]{1,0:T(8,128)(2,1)}, bf16[256,1024]{1,0:T(8,128)(2,1)}, u32[]{:S(2)}, u32[]{:S(2)}) collective-permute-start(bf16[256,1024]{1,0:T(8,128)(2,1)} %bitcast), channel_id=1, source_target_pairs={{0,1},{1,0},{2,3},{3,2},{4,5},{5,4},{6,7},{7,6},{8,9},{9,8},{10,11... | collective-permute-start | bytes 1572872 | tf_op jit(solution)/shard_map/ppermute | solution.py:411
  19.7 44.8 %collective-permute-start.30 = (bf16[256,1024]{1,0:T(8,128)(2,1)}, bf16[256,1024]{1,0:T(8,128)(2,1)S(1)}, u32[]{:S(2)}, u32[]{:S(2)}) collective-permute-start(bf16[256,1024]{1,0:T(8,128)(2,1)} %bitcast.25), channel_id=1, source_target_pairs={{0,1},{1,0},{2,3},{3,2},{4,5},{5,4},{6,7},{7,6},{8,9},{9,8},{10,11... | collective-permute-start | bytes 1572872 | tf_op jit(solution)/shard_map/ppermute | solution.py:411
  54.3 52.7 %collective-permute-start.16 = (bf16[128,2304]{1,0:T(8,128)(2,1)S(1)}, bf16[128,2304]{1,0:T(8,128)(2,1)S(1)}, u32[]{:S(2)}, u32[]{:S(2)}) collective-permute-start(bf16[128,2304]{1,0:T(8,128)(2,1)S(1)} %pad_maximum_fusion.8), channel_id=1, source_target_pairs={{0,16},{2,18},{4,20},{6,22},{8,24},{10,26},{12,28},{14,30},{16,0},... | collective-permute-start | bytes 1769480 | tf_op jit(solution)/shard_map/ppermute | solution.py:408
  56.8 62.8 %collective-permute-start.21 = (bf16[128,2304]{1,0:T(8,128)(2,1)S(1)}, bf16[128,2304]{1,0:T(8,128)(2,1)S(1)}, u32[]{:S(2)}, u32[]{:S(2)}) collective-permute-start(bf16[128,2304]{1,0:T(8,128)(2,1)S(1)} %pad_maximum_fusion.9), channel_id=1, source_target_pairs={{0,16},{2,18},{4,20},{6,22},{8,24},{10,26},{12,28},{14,30},{16,0},... | collective-permute-start | bytes 1769480 | tf_op jit(solution)/shard_map/ppermute | solution.py:408
  57.5 74.8 %collective-permute-start.26 = (bf16[128,2304]{1,0:T(8,128)(2,1)S(1)}, bf16[128,2304]{1,0:T(8,128)(2,1)S(1)}, u32[]{:S(2)}, u32[]{:S(2)}) collective-permute-start(bf16[128,2304]{1,0:T(8,128)(2,1)S(1)} %pad_maximum_fusion.10), channel_id=1, source_target_pairs={{0,16},{2,18},{4,20},{6,22},{8,24},{10,26},{12,28},{14,30},{16,0},... | collective-permute-start | bytes 1769480 | tf_op jit(solution)/shard_map/ppermute | solution.py:408
  64.5 72.8 %collective-permute-start.4 = (bf16[256,1152]{1,0:T(8,128)(2,1)S(1)}, bf16[256,1152]{1,0:T(8,128)(2,1)S(1)}, u32[]{:S(2)}, u32[]{:S(2)}) collective-permute-start(bf16[256,1152]{1,0:T(8,128)(2,1)S(1)} %pad_maximum_fusion.7), channel_id=1, source_target_pairs={{0,2},{2,0},{4,6},{6,4},{8,10},{10,8},{12,14},{14,12},{16,18},{18,... | collective-permute-start | bytes 1769480 | tf_op jit(solution)/shard_map/ppermute | solution.py:408
  72.0 68.6 %collective-permute-start.13 = (bf16[1024,512]{1,0:T(8,128)(2,1)S(1)}, bf16[1024,512]{1,0:T(8,128)(2,1)}, u32[]{:S(2)}, u32[]{:S(2)}) collective-permute-start(bf16[1024,512]{1,0:T(8,128)(2,1)S(1)} %constant_dynamic-update-slice_fusion.7), channel_id=1, source_target_pairs={{0,1},{1,0},{2,3},{3,2},{4,5},{5,4},{6,7},{7,6},{8,9},{9,8},{10,11... | collective-permute-start | bytes 3145736 | tf_op jit(solution)/shard_map/ppermute | solution.py:411
  108.1 40.8 %collective-permute-start.17 = (bf16[256,2304]{1,0:T(8,128)(2,1)}, bf16[256,2304]{1,0:T(8,128)(2,1)}, u32[]{:S(2)}, u32[]{:S(2)}) collective-permute-start(bf16[256,2304]{1,0:T(8,128)(2,1)} %pad_maximum_fusion.4), channel_id=1, source_target_pairs={{0,2},{2,0},{4,6},{6,4},{8,10},{10,8},{12,14},{14,12},{16,18},{18,... | collective-permute-start | bytes 3538952 | tf_op jit(solution)/shard_map/ppermute | solution.py:408
  133.4 49.7 %collective-permute-start.27 = (bf16[256,2304]{1,0:T(8,128)(2,1)}, bf16[256,2304]{1,0:T(8,128)(2,1)}, u32[]{:S(2)}, u32[]{:S(2)}) collective-permute-start(bf16[256,2304]{1,0:T(8,128)(2,1)} %pad_maximum_fusion.6), channel_id=1, source_target_pairs={{0,2},{2,0},{4,6},{6,4},{8,10},{10,8},{12,14},{14,12},{16,18},{18,... | collective-permute-start | bytes 3538952 | tf_op jit(solution)/shard_map/ppermute | solution.py:408
  138.4 56.2 %collective-permute-start.5 = (bf16[512,1152]{1,0:T(8,128)(2,1)}, bf16[512,1152]{1,0:T(8,128)(2,1)}, u32[]{:S(2)}, u32[]{:S(2)}) collective-permute-start(bf16[512,1152]{1,0:T(8,128)(2,1)} %pad_maximum_fusion.3), channel_id=1, source_target_pairs={{0,4},{2,6},{4,0},{6,2},{8,12},{10,14},{12,8},{14,10},{16,20},{18,... | collective-permute-start | bytes 3538952 | tf_op jit(solution)/shard_map/ppermute | solution.py:408
  151.8 179.6 %collective-permute-start.18 = (bf16[512,2304]{1,0:T(8,128)(2,1)}, bf16[512,2304]{1,0:T(8,128)(2,1)}, u32[]{:S(2)}, u32[]{:S(2)}) collective-permute-start(bf16[512,2304]{1,0:T(8,128)(2,1)} %pad_maximum_fusion), channel_id=1, source_target_pairs={{0,4},{2,6},{4,0},{6,2},{8,12},{10,14},{12,8},{14,10},{16,20},{18,... | collective-permute-start | bytes 7077896 | tf_op jit(solution)/shard_map/ppermute | solution.py:408
  160.7 219.1 %collective-permute-start.23 = (bf16[512,2304]{1,0:T(8,128)(2,1)}, bf16[512,2304]{1,0:T(8,128)(2,1)}, u32[]{:S(2)}, u32[]{:S(2)}) collective-permute-start(bf16[512,2304]{1,0:T(8,128)(2,1)} %pad_maximum_fusion.1), channel_id=1, source_target_pairs={{0,4},{2,6},{4,0},{6,2},{8,12},{10,14},{12,8},{14,10},{16,20},{18,... | collective-permute-start | bytes 7077896 | tf_op jit(solution)/shard_map/ppermute | solution.py:408
  186.0 177.2 %collective-permute-start.28 = (bf16[512,2304]{1,0:T(8,128)(2,1)}, bf16[512,2304]{1,0:T(8,128)(2,1)}, u32[]{:S(2)}, u32[]{:S(2)}) collective-permute-start(bf16[512,2304]{1,0:T(8,128)(2,1)} %pad_maximum_fusion.2), channel_id=1, source_target_pairs={{0,4},{2,6},{4,0},{6,2},{8,12},{10,14},{12,8},{14,10},{16,20},{18,... | collective-permute-start | bytes 7077896 | tf_op jit(solution)/shard_map/ppermute | solution.py:408
  212.7 114.3 %all-to-all-start = ((bf16[16,256,128]{2,1,0:T(8,128)(2,1)}), bf16[16,256,128]{2,1,0:T(8,128)(2,1)S(1)}, u32[]{:S(2)}, u32[]{:S(2)}) async-start(bf16[16,256,128]{2,1,0:T(8,128)(2,1)} %bitcast.186), calls=%async_computation | async-start | bytes 2097152 | tf_op jit(solution)/shard_map/all_to_all | solution.py:428
  406.3 42.4 %collective-permute-start.29 = (f32[256,1024]{1,0:T(8,128)}, f32[256,1024]{1,0:T(8,128)}, u32[]{:S(2)}, u32[]{:S(2)}) collective-permute-start(f32[256,1024]{1,0:T(8,128)} %slice_select_fusion.7), channel_id=1, source_target_pairs={{0,1},{1,0},{2,3},{3,2},{4,5},{5,4},{6,7},{7,6},{8,9},{9,8},{10,11... | collective-permute-start | bytes 3145736 | tf_op jit(solution)/shard_map/ppermute | solution.py:411
  430.9 192.6 %collective-permute-start.54 = (bf16[512,2304]{1,0:T(8,128)(2,1)}, bf16[512,2304]{1,0:T(8,128)(2,1)}, u32[]{:S(2)}, u32[]{:S(2)}) collective-permute-start(bf16[512,2304]{1,0:T(8,128)(2,1)} %slice.457), channel_id=1, source_target_pairs={{0,4},{2,6},{4,0},{6,2},{8,12},{10,14},{12,8},{14,10},{16,20},{18,... | collective-permute-start | bytes 7077896 | tf_op jit(solution)/shard_map/ppermute | solution.py:408
  432.9 197.1 %collective-permute-start.49 = (bf16[512,2304]{1,0:T(8,128)(2,1)}, bf16[512,2304]{1,0:T(8,128)(2,1)}, u32[]{:S(2)}, u32[]{:S(2)}) collective-permute-start(bf16[512,2304]{1,0:T(8,128)(2,1)} %slice.447), channel_id=1, source_target_pairs={{0,4},{2,6},{4,0},{6,2},{8,12},{10,14},{12,8},{14,10},{16,20},{18,... | collective-permute-start | bytes 7077896 | tf_op jit(solution)/shard_map/ppermute | solution.py:408
  435.5 199.3 %collective-permute-start.44 = (bf16[512,2304]{1,0:T(8,128)(2,1)}, bf16[512,2304]{1,0:T(8,128)(2,1)}, u32[]{:S(2)}, u32[]{:S(2)}) collective-permute-start(bf16[512,2304]{1,0:T(8,128)(2,1)} %slice.437), channel_id=1, source_target_pairs={{0,4},{2,6},{4,0},{6,2},{8,12},{10,14},{12,8},{14,10},{16,20},{18,... | collective-permute-start | bytes 7077896 | tf_op jit(solution)/shard_map/ppermute | solution.py:408
  441.1 152.4 %all-to-all-start.2 = ((bf16[16,128,128]{1,2,0:T(8,128)(2,1)}), bf16[16,128,128]{1,2,0:T(8,128)(2,1)S(1)}, u32[]{:S(2)}, u32[]{:S(2)}) async-start(bf16[16,128,128]{1,2,0:T(8,128)(2,1)} %bitcast.176), calls=%async_computation.2 | async-start | bytes 1048576 | tf_op jit(solution)/shard_map/all_to_all | solution.py:428
  468.8 154.0 %collective-permute-start.43 = (f32[32,512]{1,0:T(8,128)S(1)}, f32[32,512]{1,0:T(8,128)S(1)}, u32[]{:S(2)}, u32[]{:S(2)}) collective-permute-start(f32[32,512]{1,0:T(8,128)S(1)} %get-tuple-element.80), channel_id=1, source_target_pairs={{0,1},{1,0},{2,3},{3,2},{4,5},{5,4},{6,7},{7,6},{8,9},{9,8},{10,11... | collective-permute-start | bytes 196616 | tf_op jit(solution)/shard_map/ppermute | solution.py:411
  634.2 56.2 %collective-permute-start.50 = (bf16[256,2304]{1,0:T(8,128)(2,1)}, bf16[256,2304]{1,0:T(8,128)(2,1)}, u32[]{:S(2)}, u32[]{:S(2)}) collective-permute-start(bf16[256,2304]{1,0:T(8,128)(2,1)} %slice.449), channel_id=1, source_target_pairs={{0,2},{2,0},{4,6},{6,4},{8,10},{10,8},{12,14},{14,12},{16,18},{18,... | collective-permute-start | bytes 3538952 | tf_op jit(solution)/shard_map/ppermute | solution.py:408
  638.3 77.4 %collective-permute-start.45 = (bf16[256,2304]{1,0:T(8,128)(2,1)}, bf16[256,2304]{1,0:T(8,128)(2,1)}, u32[]{:S(2)}, u32[]{:S(2)}) collective-permute-start(bf16[256,2304]{1,0:T(8,128)(2,1)} %slice.439), channel_id=1, source_target_pairs={{0,2},{2,0},{4,6},{6,4},{8,10},{10,8},{12,14},{14,12},{16,18},{18,... | collective-permute-start | bytes 3538952 | tf_op jit(solution)/shard_map/ppermute | solution.py:408
  641.4 117.5 %all-to-all-start.3 = ((bf16[16,256,128]{2,1,0:T(8,128)(2,1)}), bf16[16,256,128]{2,1,0:T(8,128)(2,1)S(1)}, u32[]{:S(2)}, u32[]{:S(2)}) async-start(bf16[16,256,128]{2,1,0:T(8,128)(2,1)} %bitcast.175), calls=%async_computation.3 | async-start | bytes 2097152 | tf_op jit(solution)/shard_map/all_to_all | solution.py:428
  659.0 59.9 %collective-permute-start.56 = (bf16[128,2304]{1,0:T(8,128)(2,1)S(1)}, bf16[128,2304]{1,0:T(8,128)(2,1)S(1)}, u32[]{:S(2)}, u32[]{:S(2)}) collective-permute-start(bf16[128,2304]{1,0:T(8,128)(2,1)S(1)} %slice.461), channel_id=1, source_target_pairs={{0,16},{2,18},{4,20},{6,22},{8,24},{10,26},{12,28},{14,30},{16,0},... | collective-permute-start | bytes 1769480 | tf_op jit(solution)/shard_map/ppermute | solution.py:408
  (106 other events, 1687.0 us)

commit v2 on v1

--- a/solution.py
+++ b/solution.py
@@ -20,6 +20,7 @@
 I32 = jnp.int32
 QT = 512
 KT = 512
+TILES = 9
 VMEM_BYTES = 56 * 1024 * 1024
 
 NN = (((1,), (0,)), ((), ()))
@@ -63,56 +64,58 @@
     )
 
 
-def project_kernel(core_ref, n_ref, w_ref, gain_ref, cos_ref, sin_ref, raw_ref, out_ref):
+def project_kernel(n_parts, swaps, core_ref, x_ref, norm_gain_ref, gain_ref, cos_ref, sin_ref, *refs):
+    weights, (n_ref, raw_ref, out_ref) = refs[: 2 * n_parts], refs[2 * n_parts :]
     rows = cos_ref.shape[0]
     is_value = core_ref[0] == 1
-    raw_all = dot(n_ref[...], w_ref[...])
-    raw_ref[0] = raw_all
-    for s in range(2):
-        raw = raw_all[s * rows : (s + 1) * rows]
-        low = low_lanes(raw.shape)
-        inverse = lax.rsqrt(half_sums(raw * raw, low) * (1.0 / HEAD) + EPS)
-        normed = raw * inverse * gain_ref[...]
-        turned = normed * cos_ref[...] + half_turn(normed) * sin_ref[...]
-        kept = jnp.where(jnp.logical_or(low, jnp.logical_not(is_value)), turned, raw)
-        out_ref[0, s] = kept.astype(BF)
-
-
-def project(core, normed, weight, gain, cosine, sine):
+    x = x_ref[...].astype(F32)
+    inverse = lax.rsqrt(jnp.mean(x * x, axis=-1, keepdims=True) + EPS)
+    n_ref[...] = (x * inverse * norm_gain_ref[...]).astype(BF)
+    groups = KV_HEADS // 2
+    for half in range(2):
+        total, at = None, 0
+        for part in weights[half * n_parts : (half + 1) * n_parts]:
+            length = part.shape[0]
+            pieces = [n_ref[:, e : e + swaps[2]] for e in swaps[half][at // swaps[2] : (at + length) // swaps[2]]]
+            left = pieces[0] if len(pieces) == 1 else jnp.concatenate(pieces, axis=1)
+            term = dot(left, part[:, : groups * LANES])
+            total = term if total is None else total + term
+            at += length
+        raw_ref[:, half * groups * LANES : (half + 1) * groups * LANES] = total
+    low = low_lanes((rows, LANES))
+    turns = jnp.logical_or(low, jnp.logical_not(is_value))
+    for g in range(KV_HEADS):
+        for s in range(2):
+            raw = raw_ref[s * rows : (s + 1) * rows, g * LANES : (g + 1) * LANES]
+            inverse = lax.rsqrt(half_sums(raw * raw, low) * (1.0 / HEAD) + EPS)
+            normed = raw * inverse * gain_ref[...]
+            turned = normed * cos_ref[...] + half_turn(normed) * sin_ref[...]
+            out_ref[g, s] = jnp.where(turns, turned, raw).astype(BF)
+
+
+def project(core, x, norm_gain, gain, cosine, sine, parts, chunk, chunk_orders):
     rows = cosine.shape[0]
+    n_parts = len(parts[0])
+    swaps = ([c * chunk for c in chunk_orders[0]], [c * chunk for c in chunk_orders[1]], chunk)
     return pl.pallas_call(
-        project_kernel,
-        grid=(KV_HEADS,),
-        in_specs=[
-            in_smem(),
-            pl.BlockSpec(normed.shape, lambda g: (0, 0)),
-            pl.BlockSpec((weight.shape[0], LANES), lambda g: (0, g)),
-            pl.BlockSpec((1, LANES), lambda g: (0, 0)),
-            pl.BlockSpec((rows, LANES), lambda g: (0, 0)),
-            pl.BlockSpec((rows, LANES), lambda g: (0, 0)),
-        ],
-        out_specs=[
-            pl.BlockSpec((1, 2 * rows, LANES), lambda g: (g, 0, 0)),
-            pl.BlockSpec((1, 2, rows, LANES), lambda g: (g, 0, 0, 0)),
-        ],
+        functools.partial(project_kernel, n_parts, swaps),
+        in_specs=[in_smem()] + [in_vmem()] * (5 + 2 * n_parts),
+        out_specs=[in_vmem()] * 3,
         out_shape=[
-            jax.ShapeDtypeStruct((KV_HEADS, 2 * rows, LANES), F32),
+            jax.ShapeDtypeStruct(x.shape, BF),
+            jax.ShapeDtypeStruct((2 * rows, KV_HEADS * LANES), F32),
             jax.ShapeDtypeStruct((KV_HEADS, 2, rows, LANES), BF),
         ],
         compiler_params=params(),
-        cost_estimate=pl.CostEstimate(
-            flops=2 * normed.shape[0] * normed.shape[1] * weight.shape[1],
-            bytes_accessed=8 << 20,
-            transcendentals=0,
-        ),
-    )(core, normed, weight, gain, cosine, sine)
+        cost_estimate=pl.CostEstimate(flops=2 * x.shape[0] * x.shape[1] * KV_HEADS * LANES, bytes_accessed=8 << 20, transcendentals=0),
+    )(core, x, norm_gain, gain, cosine, sine, *parts[0], *parts[1])
 
 
 def unproject_kernel(core_ref, grad_ref, raw_ref, gain_ref, cos_ref, sin_ref, out_ref, gain_out_ref):
     rows = cos_ref.shape[0]
     is_value = core_ref[0] == 1
     for s in range(2):
-        raw = raw_ref[0, s * rows : (s + 1) * rows]
+        raw = raw_ref[s * rows : (s + 1) * rows]
         grad = grad_ref[0, s].astype(F32)
         low = low_lanes(raw.shape)
         inverse = lax.rsqrt(half_sums(raw * raw, low) * (1.0 / HEAD) + EPS)
@@ -139,7 +142,7 @@
         in_specs=[
             in_smem(),
             pl.BlockSpec((1, 2, rows, LANES), lambda g: (g, 0, 0, 0)),
-            pl.BlockSpec((1, 2 * rows, LANES), lambda g: (g, 0, 0)),
+            pl.BlockSpec((2 * rows, LANES), lambda g: (0, g)),
             pl.BlockSpec((1, LANES), lambda g: (0, 0)),
             pl.BlockSpec((rows, LANES), lambda g: (0, 0)),
             pl.BlockSpec((rows, LANES), lambda g: (0, 0)),
@@ -375,6 +378,276 @@
     )(core, kslot, qslot, lims, queries, own, other, pos, start, grads, mixed, lse)
 
 
+def feed_kernel(n_parts, chunk, chunks, blocks, has_acc, final, n_ref, nt_ref, c_ref, ct_ref, *refs):
+    parts, refs = refs[:n_parts], refs[n_parts:]
+    if has_acc:
+        (out_in_ref, back_in_ref), refs = refs[:2], refs[2:]
+    keep_ref, send_ref, out_ref, final_ref = refs[:4]
+    back_ref = refs[4] if final else final_ref
+    width = n_ref.shape[1]
+    tile = parts[0].shape[1] // 3
+    length = parts[0].shape[0]
+    places = []
+    for p in range(n_parts):
+        for at in range(0, length, chunk):
+            places.append((p, at, chunks[(p * length + at) // chunk] * chunk))
+
+    @pl.when(pl.program_id(0) == 0)
+    def _():
+        if has_acc:
+            out_ref[...] = out_in_ref[...]
+            back_ref[...] = back_in_ref[...]
+        else:
+            out_ref[...] = jnp.zeros_like(out_ref)
+            back_ref[...] = jnp.zeros_like(back_ref)
+
+    both = down = None
+    for p in range(n_parts):
+        tos = [to for q, _, to in places if q == p]
+        left_n = jnp.concatenate([n_ref[:, to : to + chunk] for to in tos], axis=1)
+        left_c = jnp.concatenate([c_ref[:, to : to + chunk] for to in tos], axis=1)
+        term = dot(left_n, parts[p][:, : 2 * tile])
+        other = dot(left_c, parts[p][:, 2 * tile :])
+        both = term if both is None else both + term
+        down = other if down is None else down + other
+    gate, up = both[:, :tile], both[:, tile:]
+    sig = 1.0 / (1.0 + jnp.exp(-gate))
+    silu = gate * sig
+    mid = (silu * up).astype(BF)
+    grad_gate = (down * up * (sig * (1.0 + gate * (1.0 - sig)))).astype(BF)
+    grad_up = (down * silu).astype(BF)
+    grads = jnp.concatenate([grad_gate, grad_up], axis=1)
+    for p in range(n_parts):
+        out = dot(mid, parts[p][:, 2 * tile :], NT)
+        back = dot(grads, parts[p][:, : 2 * tile], NT)
+        for q, at, to in places:
+            if q == p:
+                out_ref[:, to : to + chunk] += out[:, at : at + chunk]
+                back_ref[:, to : to + chunk] += back[:, at : at + chunk]
+    if final:
+
+        @pl.when(pl.program_id(0) == pl.num_programs(0) - 1)
+        def _():
+            final_ref[...] = back_ref[...].astype(BF)
+
+    unit = width // len(blocks)
+    per = 256 // unit
+    half = len(blocks) // 2
+    for k in range(0, len(blocks), per):
+        left_n = jnp.concatenate([nt_ref[b * unit : (b + 1) * unit, :] for b in blocks[k : k + per]], axis=0)
+        left_c = jnp.concatenate([ct_ref[b * unit : (b + 1) * unit, :] for b in blocks[k : k + per]], axis=0)
+        ref, row = (keep_ref, k) if k < half else (send_ref, k - half)
+        ref[row * unit : row * unit + 256, : 2 * tile] = dot(left_n, grads).astype(BF)
+        ref[row * unit : row * unit + 256, 2 * tile :] = dot(left_c, mid).astype(BF)
+
+
+def feed(n, n_t, c, c_t, parts, chunk, chunks, blocks, acc, tile, final):
+    rows, width = n.shape
+    cols = parts[0].shape[1]
+    whole = lambda shape: pl.BlockSpec(shape, lambda i: (0, 0))
+    cut = lambda height: pl.BlockSpec((height, 3 * tile), lambda i: (0, i))
+    acc = [] if acc is None else list(acc)
+    return pl.pallas_call(
+        functools.partial(feed_kernel, len(parts), chunk, chunks, blocks, bool(acc), final),
+        grid=(cols // (3 * tile),),
+        in_specs=[whole((rows, width)), whole((width, rows))] * 2
+        + [cut(p.shape[0]) for p in parts]
+        + [whole((rows, width))] * len(acc),
+        out_specs=[cut(width // 2)] * 2 + [whole((rows, width))] * 2,
+        out_shape=[jax.ShapeDtypeStruct((width // 2, cols), BF)] * 2 + [jax.ShapeDtypeStruct((rows, width), F32), jax.ShapeDtypeStruct((rows, width), BF if final else F32)],
+        scratch_shapes=[pltpu.VMEM((rows, width), F32)] if final else [],
+        compiler_params=params(),
+        cost_estimate=pl.CostEstimate(flops=18 * rows * width * cols // 3, bytes_accessed=16 << 20, transcendentals=0),
+    )(n, n_t, c, c_t, *parts, *acc)
+
+
+def prepare_kernel(
+    core_ref, table_ref, q_ref, k_ref, v_ref, o_ref, g_ref, u_ref, d_ref, ga_ref, gm_ref, flags_ref,
+    mine_q_ref, theirs_q_ref, mine_f_ref, theirs_f_ref,
+):
+    first = core_ref[0] == 0
+    owned, width = q_ref.shape
+
+    def put(mine_ref, theirs_ref, at, zero, one):
+        size = zero.shape[1]
+        mine_ref[:, at : at + size] = jnp.where(first, zero, one).astype(BF)
+        theirs_ref[:, at : at + size] = jnp.where(first, one, zero).astype(BF)
+
+    for g in range(KV_HEADS):
+        at = g * LANES
+        kv = slice(g * HEAD, (g + 1) * HEAD)
+        zero = jnp.concatenate([q_ref[:, at : at + HEAD], k_ref[:, kv]], axis=1)
+        one = jnp.concatenate([q_ref[:, at + HEAD : at + LANES], v_ref[:, kv]], axis=1)
+        put(mine_q_ref, theirs_q_ref, at, zero, one)
+    shape = (owned, owned)
+    diagonal = lax.broadcasted_iota(I32, shape, 0) == lax.broadcasted_iota(I32, shape, 1)
+    gain_a = jnp.sum(jnp.where(diagonal, ga_ref[...], 0.0), axis=1, keepdims=True)
+    gain_m = jnp.sum(jnp.where(diagonal, gm_ref[...], 0.0), axis=1, keepdims=True)
+    count = flags_ref.shape[1]
+    cols = count // owned
+    row = lax.broadcasted_iota(I32, (owned, count), 0)
+    col = lax.broadcasted_iota(I32, (owned, count), 1)
+    spread = jnp.where(col // cols == row, flags_ref[...].astype(F32), 0.0).astype(BF)
+    row = lax.broadcasted_iota(I32, (count, LANES), 0)
+    col = lax.broadcasted_iota(I32, (count, LANES), 1)
+    extra = dot(spread, jnp.where(row % cols == col - 3, 1.0, 0.0).astype(BF))
+    row = lax.broadcasted_iota(I32, (owned, LANES), 0)
+    col = lax.broadcasted_iota(I32, (owned, LANES), 1)
+    blocks = jnp.where(row == 0, table_ref[0, 0], jnp.where(row == 1, table_ref[0, 1], 0)).astype(F32)
+    extra = jnp.where(col == 0, gain_a, jnp.where(col == 1, gain_m, jnp.where(col == 2, blocks, extra)))
+    put(mine_q_ref, theirs_q_ref, width, extra, extra)
+    half = g_ref.shape[1] // 2
+    tile = half // TILES
+    for t in range(TILES):
+        for e, ref in enumerate((g_ref, u_ref, d_ref)):
+            at = t * tile
+            put(mine_f_ref, theirs_f_ref, (t * 3 + e) * tile, ref[:, at : at + tile], ref[:, half + at : half + at + tile])
+    put(mine_q_ref, theirs_q_ref, width + LANES, o_ref[:, : width // 2], o_ref[:, width // 2 :])
+
+
+def prepare(core, table, *arrays):
+    owned, width = arrays[0].shape
+    cols = 3 * arrays[4].shape[1] // 2
+    return pl.pallas_call(
+        prepare_kernel,
+        in_specs=[in_smem()] * 2 + [in_vmem()] * len(arrays),
+        out_specs=[in_vmem()] * 4,
+        out_shape=[jax.ShapeDtypeStruct((owned, width + LANES + width // 2), BF)] * 2 + [jax.ShapeDtypeStruct((owned, cols), BF)] * 2,
+        compiler_params=params(),
+    )(core, table, *arrays)
+
+
+def deliver_kernel(core_ref, a_ref, b_ref, c_ref, other_ref, gate_ref, up_ref, down_ref):
+    first = core_ref[0] == 0
+    owned, half = gate_ref.shape[0], gate_ref.shape[1] // 2
+    tile = half // TILES
+    per = TILES // 3
+    for t in range(TILES):
+        part = (a_ref, b_ref, c_ref)[t // per]
+        for e, out in enumerate((gate_ref, up_ref, down_ref)):
+            at = ((t % per) * 3 + e) * tile
+            kept = jnp.where(first, part[:owned, at : at + tile], part[owned:, at : at + tile])
+            arrived = other_ref[:, (t * 3 + e) * tile : (t * 3 + e + 1) * tile]
+            out[:, t * tile : (t + 1) * tile] = jnp.where(first, kept, arrived)
+            out[:, half + t * tile : half + (t + 1) * tile] = jnp.where(first, arrived, kept)
+
+
+def deliver(core, parts, other):
+    owned, cols = other.shape
+    return pl.pallas_call(
+        deliver_kernel,
+        in_specs=[in_smem()] + [in_vmem()] * 4,
+        out_specs=[in_vmem()] * 3,
+        out_shape=[jax.ShapeDtypeStruct((owned, 2 * cols // 3), F32)] * 3,
+        compiler_params=params(),
+    )(core, *parts, other)
+
+
+def deliver_heads_kernel(core_ref, qkv_ref, out_ref, other_ref, wo_ref, q_ref, k_ref, v_ref):
+    first = core_ref[0] == 0
+    owned, width = q_ref.shape
+    half = width // 2
+
+    def sides(ref, at, size, shift):
+        kept = jnp.where(first, ref[:owned, at : at + size], ref[owned:, at : at + size])
+        arrived = other_ref[:, shift + at : shift + at + size]
+        return jnp.where(first, kept, arrived), jnp.where(first, arrived, kept)
+
+    wo_ref[:, :half], wo_ref[:, half:] = sides(out_ref, 0, half, width)
+    for g in range(0, KV_HEADS, 2):
+        zero, one = sides(qkv_ref, g * LANES, LANES, 0)
+        zero_next, one_next = sides(qkv_ref, (g + 1) * LANES, LANES, 0)
+        q_ref[:, g * LANES : (g + 1) * LANES] = jnp.concatenate([zero[:, :HEAD], one[:, :HEAD]], axis=1)
+        q_ref[:, (g + 1) * LANES : (g + 2) * LANES] = jnp.concatenate([zero_next[:, :HEAD], one_next[:, :HEAD]], axis=1)
+        k_ref[:, g * HEAD : (g + 2) * HEAD] = jnp.concatenate([zero[:, HEAD:], zero_next[:, HEAD:]], axis=1)
+        v_ref[:, g * HEAD : (g + 2) * HEAD] = jnp.concatenate([one[:, HEAD:], one_next[:, HEAD:]], axis=1)
+
+
+def deliver_heads(core, qkv, out, other):
+    owned, width = other.shape[0], qkv.shape[1]
+    shapes = [(owned, width), (owned, width), (owned, width // 2), (owned, width // 2)]
+    return pl.pallas_call(
+        deliver_heads_kernel,
+        in_specs=[in_smem()] + [in_vmem()] * 3,
+        out_specs=[in_vmem()] * 4,
+        out_shape=[jax.ShapeDtypeStruct(e, F32) for e in shapes],
+        compiler_params=params(),
+    )(core, qkv, out, other)
+
+
+def leave_kernel(own_ref, other_ref, x_ref, wo_ref, gain_ref, res_ref, n_ref, nt_ref, attn_ref):
+    half = KV_HEADS * HEAD
+    for which, ref in enumerate((own_ref, other_ref)):
+        for g in range(0, KV_HEADS, 2):
+            for s in range(2):
+                for j in range(2):
+                    lanes = slice(j * HEAD, (j + 1) * HEAD)
+                    a = ref[(g * 2 + s) * BLOCK : (g * 2 + s + 1) * BLOCK, lanes]
+                    b = ref[((g + 1) * 2 + s) * BLOCK : ((g + 1) * 2 + s + 1) * BLOCK, lanes]
+                    row, col = (s * 2 + j) * BLOCK, which * half + g * HEAD
+                    attn_ref[row : row + BLOCK, col : col + LANES] = jnp.concatenate([a, b], axis=1)
+    value = x_ref[...].astype(F32) + dot(attn_ref[...], wo_ref[...])
+    res_ref[...] = value
+    inverse = lax.rsqrt(jnp.mean(value * value, axis=-1, keepdims=True) + EPS)
+    normed = (value * inverse * gain_ref[...]).astype(BF)
+    n_ref[...] = normed
+    nt_ref[...] = normed.T
+
+
+def leave(own, other, x, wo, gain):
+    rows, width = x.shape
+    return pl.pallas_call(
+        leave_kernel,
+        in_specs=[in_vmem()] * 5,
+        out_specs=[in_vmem()] * 4,
+        out_shape=[
+            jax.ShapeDtypeStruct((rows, width), F32),
+            jax.ShapeDtypeStruct((rows, width), BF),
+            jax.ShapeDtypeStruct((width, rows), BF),
+            jax.ShapeDtypeStruct((rows, width), BF),
+        ],
+        compiler_params=params(),
+        cost_estimate=pl.CostEstimate(flops=2 * rows * width * width, bytes_accessed=10 << 20, transcendentals=0),
+    )(own, other, x, wo, gain)
+
+
+def enter_kernel(back_ref, other_ref, res_ref, c_ref, gain_ref, wo_ref, grad_ref, grad_b_ref, gain_out_ref, out_ref):
+    value = res_ref[...]
+    inverse = lax.rsqrt(jnp.mean(value * value, axis=-1, keepdims=True) + EPS)
+    grad = back_ref[...].astype(F32) + other_ref[...].astype(F32)
+    gain_out_ref[...] = jnp.sum(grad * value * inverse, axis=0, keepdims=True)
+    scaled = grad * gain_ref[...]
+    mean = jnp.mean(scaled * value, axis=-1, keepdims=True)
+    total = c_ref[...].astype(F32) + (inverse * scaled - value * (inverse * inverse * inverse) * mean)
+    grad_ref[...] = total
+    grad_b_ref[...] = total.astype(BF)
+    heads = dot(grad_b_ref[...], wo_ref[: KV_HEADS * HEAD, :], NT).astype(BF)
+    for g in range(KV_HEADS):
+        for s in range(2):
+            row = s * 2 * BLOCK
+            lanes = slice(g * HEAD, (g + 1) * HEAD)
+            out_ref[(g * 2 + s) * BLOCK : (g * 2 + s + 1) * BLOCK, :] = jnp.concatenate(
+                [heads[row : row + BLOCK, lanes], heads[row + BLOCK : row + 2 * BLOCK, lanes]], axis=1
+            )
+
+
+def enter(back, other, residual, c, gain, wo):
+    rows, width = residual.shape
+    return pl.pallas_call(
+        enter_kernel,
+        in_specs=[in_vmem()] * 6,
+        out_specs=[in_vmem()] * 4,
+        out_shape=[
+            jax.ShapeDtypeStruct((rows, width), F32),
+            jax.ShapeDtypeStruct((rows, width), BF),
+            jax.ShapeDtypeStruct((1, width), F32),
+            jax.ShapeDtypeStruct((2 * KV_HEADS * BLOCK, LANES), BF),
+        ],
+        compiler_params=params(),
+        cost_estimate=pl.CostEstimate(flops=rows * width * width, bytes_accessed=10 << 20, transcendentals=0),
+    )(back, other, residual, c, gain, wo)
+
+
 def rms(value, gain):
     inverse = lax.rsqrt(jnp.mean(value * value, axis=-1, keepdims=True) + EPS)
     return value * inverse * gain, inverse
@@ -397,32 +670,124 @@
     )
 
 
+class Dim:
+    def __init__(self, stride, size):
+        self.stride, self.size = stride, size
+
+
 def make_shards(n):
-    bits = n.bit_length() - 1
-    order = [4, 8, 1, 2] if n == 16 else [1 << b for b in range(bits)]
+    if n == 16:
+        dims = {"x": Dim(1, 2), "y": Dim(2, 2), "p": Dim(4, 2), "q": Dim(8, 2)}
+        order_a, order_b, order_c = "qpxy", "qpyx", "qxyp"
+    else:
+        names = "abcdefghijkl"[: n.bit_length() - 1]
+        dims = {name: Dim(1 << b, 2) for b, name in enumerate(names)}
+        order_a = order_b = order_c = names
     groups = n // 16
     a2a_groups = None if groups == 1 else [[t * 16 + d for d in range(16)] for t in range(groups)]
     kv_groups = None if groups == 1 else [[t * 16 + d for t in range(groups)] for d in range(16)]
 
-    def ctx_swap(value, mask):
-        return lax.ppermute(value, "ctx", [(i, i ^ mask) for i in range(n)])
+    def digits(order):
+        places = []
+        for r in range(n):
+            place = {}
+            for name in order:
+                place[name] = r % dims[name].size
+                r //= dims[name].size
+            places.append(place)
+        return places
+
+    def place_in(order):
+        found = {tuple(sorted(p.items())): r for r, p in enumerate(digits(order))}
+        return [found[tuple(sorted(p.items()))] for p in digits(order_a)]
+
+    def chips(me, order):
+        out = []
+        for place in digits(order):
+            chip = me
+            for name, digit in place.items():
+                d = dims[name]
+                at = (me // d.stride) % d.size
+                to = jnp.bitwise_xor(at, digit)
+                chip = chip + (to - at) * d.stride
+            out.append(chip)
+        return jnp.stack(out).astype(I32)
+
+    def ctx_send(value, pairs):
+        return lax.ppermute(value, "ctx", pairs)
+
+    def ctx_swap(value, stride):
+        return ctx_send(value, [(i, i ^ stride) for i in range(n)])
 
     def core_swap(value):
         return lax.ppermute(value, "wt", [(0, 1), (1, 0)])
 
-    def gather_rows(piece):
-        for mask in order:
-            piece = jnp.concatenate([piece, ctx_swap(piece, mask)], axis=0)
-        return piece
-
-    def scatter_rows(value):
-        for level, mask in enumerate(reversed(order)):
-            half = value.shape[0] // 2
-            arrived = ctx_swap(value[half:], mask)
-            value = value[:half].astype(F32) + arrived.astype(F32)
-            if level < len(order) - 1:
-                value = value.astype(BF)
-        return value
+    def gather_dim(value, name):
+        return [value, ctx_swap(value, dims[name].stride)]
+
+    def join(parts):
+        return parts[0] if len(parts) == 1 else jnp.concatenate(parts, axis=0)
+
+    def gather_rows(parts, names):
+        for name in names:
+            parts = gather_dim(join(parts), name)
+        return parts
+
+    def hold(parts, *others):
+        return parts[:-1] + [after(parts[-1], *others)]
+
+    def scatter_begin(keep, send, name):
+        return keep, ctx_swap(send.astype(BF), dims[name].stride)
+
+    def scatter_next(state, name):
+        keep, arrived = state
+        half = keep.shape[0] // 2
+        send = (keep[half:].astype(F32) + arrived[half:].astype(F32)).astype(BF)
+        return keep[:half].astype(F32) + arrived[:half].astype(F32), ctx_swap(send, dims[name].stride)
+
+    def scatter_end(state):
+        keep, arrived = state
+        return keep.astype(F32) + arrived.astype(F32)
+
+    def scatter_rows(keep, send, names):
+        state = scatter_begin(keep, send, names[-1])
+        for name in reversed(names[:-1]):
+            state = scatter_next(state, name)
+        return scatter_end(state)
+
+    def scatter_whole(value, names):
+        half = value.shape[0] // 2
+        return scatter_rows(value[:half], value[half:], names)
+
+    def runs(places):
+        out = []
+        for p in places:
+            if out and out[-1][1] == p:
+                out[-1][1] = p + 1
+            else:
+                out.append([p, p + 1])
+        return out
+
+    def assemble(parts, order):
+        total = sum(p.shape[0] for p in parts)
+        unit, each = total // n, parts[0].shape[0] // (total // n)
+        out = []
+        for lo, hi in runs(place_in(order)):
+            while lo < hi:
+                part, at = lo // each, lo % each
+                stop = min(hi, (part + 1) * each)
+                out.append(parts[part][at * unit : (at + stop - lo) * unit])
+                lo = stop
+        return join(out)
+
+    def columns_in(value, order):
+        unit = value.shape[1] // n
+        inverse = np.argsort(place_in(order)).tolist()
+        pieces = [value[:, lo * unit : hi * unit] for lo, hi in runs(inverse)]
+        return pieces[0] if len(pieces) == 1 else jnp.concatenate(pieces, axis=1)
+
+    def after(value, *others):
+        return lax.optimization_barrier((value,) + others)[0]
 
     def swap_heads(value):
         return lax.all_to_all(value, "ctx", 0, 0, axis_index_groups=a2a_groups, tiled=True)
@@ -447,51 +812,73 @@
         def pick(a, b):
             return jnp.where(first, a, b)
 
-        rel = np.arange(n)
-        offset = sum(((rel >> level) & 1) * mask for level, mask in enumerate(order))
-        chip_of = jnp.bitwise_xor(me.astype(I32), jnp.asarray(offset, I32))
-        canon = (chip_of[:, None] * chip_rows + jnp.arange(chip_rows, dtype=I32)[None, :]).reshape(-1)
-        perm = (jnp.arange(width, dtype=I32)[:, None] == canon[None, :]).astype(BF)
-
-        def chip_piece(zero, one):
-            mine = pick(zero, one).astype(BF)
-            theirs = pick(one, zero).astype(BF)
-            return by_core(mine, core_swap(theirs))
-
-        def halves(weight):
-            half = weight.shape[1] // 2
-            return chip_piece(weight[:, :half], weight[:, half:])
-
-        q_pairs = w_query.reshape(owned, KV_HEADS, 2, HEAD)
-        qk = jnp.concatenate([q_pairs[:, :, 0], key_weight.reshape(owned, KV_HEADS, HEAD)], axis=-1).reshape(owned, width)
-        qv = jnp.concatenate([q_pairs[:, :, 1], value_weight.reshape(owned, KV_HEADS, HEAD)], axis=-1).reshape(owned, width)
+        chip_of = chips(me, order_a)
+
+        def features(order):
+            return (chips(me, order)[:, None] * chip_rows + jnp.arange(chip_rows, dtype=I32)[None, :]).reshape(-1)
+
+        def spread(order):
+            return (jnp.arange(width, dtype=I32)[:, None] == features(order)[None, :]).astype(BF)
+
+        canon = features(order_a)
+        perm = spread(order_a)
+
         flag_cols = rows // owned
         own_blocks = block_table[0]
-        table_col = jnp.concatenate([own_blocks.astype(F32), jnp.zeros((owned - 2,), F32)])
-        extra = jnp.concatenate(
+        mine_q, theirs_q, mine_f, theirs_f = prepare(
+            core_arr, block_table, w_query, key_weight, value_weight, w_out, w_gate, w_up, w_down,
+            gain_attn[None, :], gain_mlp[None, :], doc_flags,
+        )
+        first_piece = by_core(mine_q, core_swap(theirs_q))
+        acts = jnp.stack([tokens[0], cotangent[0]])
+        acts_other = core_swap(acts)
+        other_f = core_swap(theirs_f)
+        x_two = dot(by_core(acts[0], acts_other[0]), perm).astype(BF)
+        c_two = dot(by_core(acts[1], acts_other[1]), perm).astype(BF)
+        head_cols = width // 2
+        out_cols = width // 4
+        out_at = width + LANES
+
+        def cut(value):
+            first_cols = [value[:, :head_cols], value[:, width:out_at], value[:, out_at : out_at + out_cols]]
+            second_cols = [value[:, head_cols:width], value[:, out_at + out_cols :]]
+            return [jnp.concatenate(first_cols, axis=1)], [jnp.concatenate(second_cols, axis=1)]
+
+        if n == 16:
+            shared = cut(join(gather_rows([first_piece], "qp")))
+            qkv_parts = [gather_rows(shared[0], "x"), gather_rows(shared[1], "y")]
+            first_swap = qkv_parts[0][-1]
+            qkv_parts = [gather_rows(hold(qkv_parts[0], x_two), "y"), gather_rows(qkv_parts[1], "x")]
+        else:
+            shared = cut(first_piece)
+            qkv_parts = [gather_rows(shared[0], order_a), gather_rows(shared[1], order_b)]
+            first_swap = first_piece
+        chunk = LANES
+        per = chunk // chip_rows
+        chunk_orders = [[e // per for e in np.argsort(place_in(o)).tolist()[::per]] for o in (order_a, order_b, order_c)]
+        extras = assemble([p[:, head_cols : head_cols + LANES] for p in qkv_parts[0]], order_a).astype(F32)
+        wo_half = jnp.concatenate(
             [
-                gain_attn[:, None],
-                gain_mlp[:, None],
-                table_col[:, None],
-                doc_flags[0].reshape(owned, flag_cols).astype(F32),
-                jnp.zeros((owned, LANES - 3 - flag_cols), F32),
+                assemble([p[:, head_cols + LANES :] for p in qkv_parts[0]], order_a),
+                assemble([p[:, head_cols:] for p in qkv_parts[1]], order_b),
             ],
             axis=1,
         )
-        first_piece = chip_piece(jnp.concatenate([qk, extra], axis=1), jnp.concatenate([qv, extra], axis=1))
-        first_full = gather_rows(first_piece)
-        w_qkv = first_full[:, :width]
-        extras = first_full[:, width:].astype(F32)
-
-        x_own, c_own = tokens[0], cotangent[0]
-        x_two = dot(by_core(x_own, core_swap(x_own)), perm).astype(BF)
-        c_two = dot(by_core(c_own, core_swap(c_own)), perm).astype(BF)
+
         hidden = x_two.astype(F32)
 
-        wo_half = gather_rows(halves(w_out))
-        w_g = gather_rows(halves(w_gate))
-        w_u = gather_rows(halves(w_up))
-        w_d = gather_rows(halves(w_down))
+        ff_half = w_gate.shape[1] // 2
+        tile = ff_half // TILES
+        piece_cols = ff_half
+        orders = (order_a, order_b, order_c)
+        other_f = after(other_f, first_swap)
+
+        def feed_piece(lo, hi):
+            return by_core(mine_f[:, lo:hi], other_f[:, lo:hi])
+
+        feed_parts = [
+            gather_rows([feed_piece(e * piece_cols, (e + 1) * piece_cols)], orders[e][:1]) for e in range(3)
+        ]
 
         gain_a, gain_m = extras[:, 0][None, :], extras[:, 1][None, :]
         per_chip = extras.reshape(n, 2, owned, LANES)
@@ -529,24 +916,15 @@
         cosine, sine = rope_tables(own_pos)
         gain_qk = jnp.concatenate([gain_q, key_norm_gain])[None, :]
 
-        normed_a, inv_a = rms(hidden, gain_a)
-        normed_ab = normed_a.astype(BF)
-        raw, packed = project(core_arr, normed_ab, w_qkv, gain_qk, cosine, sine)
+        normed_ab, raw, packed = project(
+            core_arr, x_two, gain_a, gain_qk, cosine, sine, qkv_parts, chunk, chunk_orders
+        )
+        feed_parts = [gather_rows(hold(feed_parts[e], packed), orders[e][1:]) for e in range(3)]
         queries = swap_heads(packed.reshape(16, rows, LANES)).reshape(n_q, LANES)
         own_kv = queries
         if groups > 1:
             own_kv = lax.all_gather(queries, "ctx", axis=0, tiled=True, axis_index_groups=kv_groups)
         other_kv = core_swap(own_kv)
-        mixed_packed, mixed, lse = attend(core_arr, tables, queries, own_kv, other_kv)
-
-        def heads_to_rows(value):
-            value = value.reshape(KV_HEADS, 2, BLOCK, 2, HEAD)
-            return jnp.transpose(value, (1, 3, 2, 0, 4)).reshape(2 * rows, KV_HEADS * HEAD)
-
-        def rows_to_heads(value):
-            value = value.reshape(2, 2, BLOCK, KV_HEADS, HEAD)
-            return jnp.transpose(value, (3, 0, 2, 1, 4)).reshape(16, BLOCK, LANES)
-
         wo_other = core_swap(wo_half)
         wo_full = by_core(wo_half, wo_other, axis=1)
         head_ids = jnp.arange(width, dtype=I32)
@@ -555,97 +933,120 @@
         select = (head_row[:, None] == canon[None, :]).astype(BF)
         wo_sel = dot(select, dot(wo_full, perm).astype(BF)).astype(BF)
 
-        attn_own = heads_to_rows(swap_heads(mixed_packed.reshape(16, BLOCK, LANES)))
-        attn = jnp.concatenate([attn_own, core_swap(attn_own)], axis=1)
-        residual = hidden + dot(attn, wo_sel)
-        normed_m, inv_m = rms(residual, gain_m)
-        normed_mb = normed_m.astype(BF)
-
-        gate = dot(normed_mb, w_g)
-        up = dot(normed_mb, w_u)
-        sig = jax.nn.sigmoid(gate)
-        silu = gate * sig
-        mid = (silu * up).astype(BF)
-        grad_mid = dot(c_two, w_d)
-        grad_gate_in = (grad_mid * up * (sig * (1.0 + gate * (1.0 - sig)))).astype(BF)
-        grad_up_in = (grad_mid * silu).astype(BF)
-        grad_n2_part = (dot(grad_gate_in, w_g, NT) + dot(grad_up_in, w_u, NT)).astype(BF)
-        grad_n2 = grad_n2_part.astype(F32) + core_swap(grad_n2_part).astype(F32)
-        moved_m, grad_gm = rms_back(residual, inv_m, gain_m, grad_n2)
-        grad_h = c_two.astype(F32) + moved_m
-        grad_hb = grad_h.astype(BF)
-        grad_attn = dot(grad_hb, wo_sel[: KV_HEADS * HEAD], NT).astype(BF)
-        grads_in = swap_heads(rows_to_heads(grad_attn)).reshape(n_q // 2, LANES)
-
-        mlp_part = dot(mid, w_d, NT)
+        other_kv = after(other_kv, wo_sel)
+        mixed_packed, mixed, lse = attend(core_arr, tables, queries, own_kv, other_kv)
+
+        attn_own = swap_heads(mixed_packed.reshape(16, BLOCK, LANES)).reshape(16 * BLOCK, LANES)
+        residual, normed_mb, n_t, attn = leave(attn_own, core_swap(attn_own), x_two, wo_sel, gain_m)
+
+        c_t = c_two.T
+        acc, feed_sums = None, []
+        for e in range(3):
+            blocks = np.argsort(place_in(orders[e])).tolist()
+            keep, send, *acc = feed(
+                normed_mb, n_t, c_two, c_t, feed_parts[e], chunk, chunk_orders[e], blocks, acc, tile, e == 2
+            )
+            feed_sums.append(scatter_begin(keep, send, orders[e][-1]))
+        mlp_part, grad_n2_part = acc
+        grad_h, grad_hb, grad_gm, do_packed = enter(
+            grad_n2_part, core_swap(grad_n2_part), residual, c_two, gain_m, wo_sel
+        )
+        grads_in = swap_heads(do_packed.reshape(16, BLOCK, LANES)).reshape(n_q // 2, LANES)
+        attn = after(attn, do_packed)
+
         mlp_other = core_swap(pick(mlp_part[rows:], mlp_part[:rows]))
         layer_rel = pick(residual[:rows], residual[rows:]) + (pick(mlp_part[:rows], mlp_part[rows:]) + mlp_other)
         layer_out = dot(layer_rel.astype(BF), perm, NT).astype(BF)[None]
 
-        part_down = scatter_rows(dot(c_two, mid, TN).astype(BF))
-        part_gate = scatter_rows(dot(normed_mb, grad_gate_in, TN).astype(BF))
-        part_up = scatter_rows(dot(normed_mb, grad_up_in, TN).astype(BF))
         attn_rel = dot(attn, select).astype(BF)
         grad_hc = dot(grad_hb, pick(perm[: width // 2], perm[width // 2 :]), NT).astype(BF)
-        part_out = scatter_rows(dot(attn_rel, grad_hc, TN).astype(BF))
+        out_first = dot(attn_rel, grad_hc[:, :out_cols], TN).astype(BF)
+        out_second = dot(columns_in(attn_rel, order_b), grad_hc[:, out_cols:], TN).astype(BF)
 
         dq, keep, send = attend_back(core_arr, tables, queries, own_kv, other_kv, grads_in, mixed, lse)
+        feed_sums = [scatter_next(hold(list(feed_sums[e]), send), orders[e][-2]) for e in range(3)]
         grad_kv = keep + core_swap(send).astype(F32)
         if groups > 1:
             grad_kv = lax.psum_scatter(grad_kv, "ctx", scatter_dimension=0, tiled=True, axis_index_groups=kv_groups)
         back = swap_heads((dq + grad_kv).astype(BF).reshape(16, rows, LANES))
         grad_qkv_in, gain_parts = unproject(core_arr, back.reshape(KV_HEADS, 2, rows, LANES), raw, gain_qk, cosine, sine)
-        part_qkv = scatter_rows(dot(normed_ab, grad_qkv_in, TN).astype(BF))
-        n1_part = dot(grad_qkv_in, w_qkv, NT)
+        g_first, g_second = grad_qkv_in[:, : width // 2], grad_qkv_in[:, width // 2 :]
+
+        def halves(value):
+            half = value.shape[0] // 2
+            return value[:half], value[half:]
+
+        sum_first = jnp.concatenate([dot(normed_ab, g_first, TN).astype(BF), out_first], axis=1)
+        sum_second = jnp.concatenate([dot(columns_in(normed_ab, order_b), g_second, TN).astype(BF), out_second], axis=1)
+        level_holds = {}
+        if n == 16:
+            sum_first = scatter_begin(*halves(sum_first), "y")
+            sum_second = scatter_begin(*halves(sum_second), "x")
+            level_holds[3] = sum_first[1], sum_second[1]
+            sum_first = scatter_next(sum_first, "x")
+            sum_second = scatter_next(sum_second, "y")
+            level_holds[4] = sum_first[1], sum_second[1]
+            sums = jnp.concatenate([scatter_end(sum_first), scatter_end(sum_second)], axis=1)
+            sums = scatter_whole(sums, "qp")
+        else:
+            sums = jnp.concatenate([scatter_whole(sum_first, order_a), scatter_whole(sum_second, order_b)], axis=1)
+        cut_cols = head_cols + out_cols
+        part_qkv = jnp.concatenate([sums[:, :head_cols], sums[:, cut_cols : cut_cols + head_cols]], axis=1)
+        part_out = jnp.concatenate([sums[:, head_cols:cut_cols], sums[:, cut_cols + head_cols :]], axis=1)
+        w_first = assemble([p[:, : width // 2] for p in qkv_parts[0]], order_a)
+        w_second = assemble([p[:, : width // 2] for p in qkv_parts[1]], order_b)
+        n1_part = dot(g_first, w_first, NT) + dot(g_second, w_second, NT)
         n1_other = core_swap(pick(n1_part[rows:], n1_part[:rows]))
         grad_n1 = pick(n1_part[:rows], n1_part[rows:]) + n1_other
 
         def mine(value):
             return pick(value[:rows], value[rows:])
 
-        moved_a, grad_ga = rms_back(mine(hidden), mine(inv_a), gain_a, grad_n1)
+        x_mine = mine(hidden)
+        _, inv_a = rms(x_mine, gain_a)
+        moved_a, grad_ga = rms_back(x_mine, inv_a, gain_a, grad_n1)
         grad_in_rel = mine(grad_h) + moved_a
         in_hi = grad_in_rel.astype(BF)
         in_lo = (grad_in_rel - in_hi.astype(F32)).astype(BF)
         grad_input = (dot(in_hi, perm, NT) + dot(in_lo, perm, NT))[None]
 
-        vectors = jnp.stack([grad_ga, jnp.where(first, grad_gm, 0.0)])
+        vectors = jnp.stack([grad_ga, jnp.where(first, grad_gm[0], 0.0)])
         vectors = lax.dot_general(
             vectors, perm.astype(F32), NT, precision=lax.Precision.HIGHEST, preferred_element_type=F32
         )
+        for level in range(3, len(order_a) + 1):
+            if level == 3:
+                feed_sums = [hold(list(v), *level_holds.get(3, (grad_qkv_in,))) for v in feed_sums]
+            if level == 4:
+                feed_sums = [hold(list(v), vectors, *level_holds.get(4, ())) for v in feed_sums]
+            feed_sums = [scatter_next(feed_sums[e], orders[e][-level]) for e in range(3)]
+        feed_sums = [scatter_end(v) for v in feed_sums]
         heads_gain = jnp.sum(gain_parts[:, 0], axis=0)
         small = jnp.concatenate([vectors.reshape(-1, LANES), heads_gain[None], jnp.zeros((7, LANES), F32)])
-        for mask in order:
-            small = small + ctx_swap(small, mask)
+        for bit in range(n.bit_length() - 1):
+            small = small + ctx_swap(small, 1 << bit)
         small = small + core_swap(small)
         my_row = (me * 2 + core) * owned
         gains = small[: 2 * width // LANES].reshape(2, width)
         gains = lax.dynamic_slice_in_dim(gains, my_row, owned, axis=1)
 
-        def finish(part):
-            kept = pick(part[:owned], part[owned:])
-            arrived = core_swap(pick(part[owned:], part[:owned]))
-            return kept, arrived
-
-        def finish_halves(part):
-            return by_core(*finish(part), axis=1)
-
-        kept, arrived = finish(part_qkv)
-        zero = pick(kept, arrived).reshape(owned, KV_HEADS, LANES)
-        one = pick(arrived, kept).reshape(owned, KV_HEADS, LANES)
-        grad_query = jnp.stack([zero[..., :HEAD], one[..., :HEAD]], axis=2).reshape(owned, width)
-        grad_key = zero[..., HEAD:].reshape(owned, KV_HEADS * HEAD)
-        grad_value = one[..., HEAD:].reshape(owned, KV_HEADS * HEAD)
+        def theirs(parts):
+            return jnp.concatenate([pick(p[owned:], p[:owned]) for p in parts], axis=1)
+
+        grad_gate, grad_up, grad_down = deliver(core_arr, feed_sums, core_swap(theirs(feed_sums)))
+        grad_wout, grad_query, grad_key, grad_value = deliver_heads(
+            core_arr, part_qkv, part_out, core_swap(theirs([part_qkv, part_out]))
+        )
         return (
             layer_out,
             grad_input,
             grad_query,
             grad_key,
             grad_value,
-            finish_halves(part_out),
-            finish_halves(part_gate),
-            finish_halves(part_up),
-            finish_halves(part_down),
+            grad_wout,
+            grad_gate,
+            grad_up,
+            grad_down,
             gains[0],
             gains[1],
             small[2 * width // LANES, :HEAD],

time: 862 us -> 612 us (0.71)
  waiting for transfers between devices: 482 us -> 258 us
  Pallas kernels: 63 us -> 131 us
  matrix products: 74.1 us -> 30.8 us
  local copies, waits for them, and re-layouts: 61 us -> 22.9 us
  starting transfers between devices: 103 us -> 85.3 us
  other arithmetic: 63 us -> 74.9 us
    all_to_all x4, waiting for transfers between devices: 227 us -> 93.1 us  [swap_heads(): lax.all_to_all(value, 'ctx', 0, 0, axis_index_groups=a2a_groups, tiled=True)]
    ppermute x44 -> x40, waiting for transfers between devices: 255 us -> 165 us  [ctx_send(): return lax.ppermute(value, 'ctx', pairs)]
    pallas_call x1 -> x9, Pallas kernels: 9.76 us -> 70.7 us  [the longest x3 43.6 us: feed(): pl.pallas_call(functools.partial(feed_kernel, len(parts), chunk, chunks,...]
    dot_general x22 -> x15, matrix products: 72.2 us -> 28.3 us  [dot(): return lax.dot_general(a, b, dims, preferred_element_type=F32)]
    unnamed x145 -> x181, local copies, waits for them, and re-layouts: 19.6 us -> 6.42 us
    concatenate x8 -> x0, local copies, waits for them, and re-layouts: 12.4 us -> none  [the longest x5 12.1 us: gather_rows(): piece = jnp.concatenate([piece, ctx_swap(piece, mask)], axis=0)]
    ppermute x20 -> x13, starting transfers between devices: 26.7 us -> 16.3 us  [core_swap(): return lax.ppermute(value, 'wt', [(0, 1), (1, 0)])]
    concatenate x17 -> x22, other arithmetic: 13.5 us -> 20 us  [the longest x13 17.3 us: join(): return parts[0] if len(parts) == 1 else jnp.concatenate(parts, axis=0)]
  transfers between devices with their start and end apart: 68 -> 57, of which waited for: 29 -> 22; matrix products, arithmetic and copies ran while one was open for 20% -> 20% of each run, Pallas kernels for 7% -> 18%
where the time goes in v2:
time: 612 us; the launch traced here: 605 us
  waiting for transfers between devices  258 us (42%)
  Pallas kernels  131 us (21%)
  starting transfers between devices  85.3 us (14%)
  other arithmetic  74.9 us (12%)
  matrix products  30.8 us (5%)
  local copies, waits for them, and re-layouts  22.9 us (4%)
    ppermute x40, waiting for transfers between devices, ctx_send(): return lax.ppermute(value, 'ctx', pairs)  165 us
    all_to_all x4, waiting for transfers between devices, swap_heads(): lax.all_to_all(value, 'ctx', 0, 0, axis_index_groups=a2a_groups, tiled=True)  93.1 us
    ppermute x40, starting transfers between devices, ctx_send(): return lax.ppermute(value, 'ctx', pairs)  48.2 us
    pallas_call x3, Pallas kernels, feed(): pl.pallas_call(functools.partial(feed_kernel, len(parts), chunk, chunks,...  43.6 us
    pallas_call x1, Pallas kernels, attend_back(): pl.pallas_call(attend_back_kernel, in_specs=[in_smem()] * 4 + [in_vmem()]...  32 us
    dot_general x15, matrix products, dot(): return lax.dot_general(a, b, dims, preferred_element_type=F32)  28.3 us
    convert_element_type x12, other arithmetic, scatter_next(): send = (keep[half:].astype(F32) + arrived[half:].astype(F32)).astype(BF)  26.9 us
    all_to_all x4, starting transfers between devices, swap_heads(): lax.all_to_all(value, 'ctx', 0, 0, axis_index_groups=a2a_groups, tiled=True)  20.8 us
  transfers between devices with their start and end apart: 57, of which 22 were waited for; matrix products, arithmetic and copies ran while one was open for 20% of the time, Pallas kernels for 18%

profile of v2, /device:TPU:1, one launch (start us, length us, event | category | flops | bytes accessed | tf_op | source)
XLA Modules:
  0.0 605.3 jit_solution(16046180791356430875)
XLA Ops:
  13.6 8.5 %collective-permute-done.1 = bf16[64,1664]{1,0:T(8,128)(2,1)S(1)} collective-permute-done((bf16[64,1664]{1,0:T(8,128)(2,1)S(1)}, bf16[64,1664]{1,0:T(8,128)(2,1)S(1)}, u32[]{:S(2)}, u32[]{:S(2)}) %collective-permute-start.1) | collective-permute-done | bytes 213024 | tf_op jit(solution)/shard_map/ppermute | solution.py:717
  23.0 10.0 %collective-permute-done.2 = bf16[128,1664]{1,0:T(8,128)(2,1)S(1)} collective-permute-done((bf16[128,1664]{1,0:T(8,128)(2,1)S(1)}, bf16[128,1664]{1,0:T(8,128)(2,1)S(1)}, u32[]{:S(2)}, u32[]{:S(2)}) %collective-permute-start.2) | collective-permute-done | bytes 426016 | tf_op jit(solution)/shard_map/ppermute | solution.py:717
  52.6 9.4 %collective-permute-done.7.refs_3_ = bf16[512,768]{1,0:T(8,128)(2,1)S(1)} collective-permute-done((bf16[512,768]{1,0:T(8,128)(2,1)S(1)}, bf16[512,768]{1,0:T(8,128)(2,1)S(1)}, u32[]{:S(2)}, u32[]{:S(2)}) %collective-permute-start.7) | collective-permute-done | bytes 786464 | tf_op jit(solution)/shard_map/ppermute | solution.py:717
  63.3 7.4 %shard_map.247 = (bf16[512,1024]{1,0:T(8,128)(2,1)}, f32[512,1024]{1,0:T(8,128)}, bf16[8,2,256,128]{3,2,1,0:T(8,128)(2,1)}) custom-call(s32[1]{0:T(128)} %bitcast.core_ref, bf16[512,1024]{1,0:T(8,128)(2,1)} %get-tuple-element.196.x_ref, f32[1,1024]{1,0:T(1,128)} %bitcast.143, f32[1,128]{1,0:T(1,128)} %maximum_bitcast_fusion.gain_ref, ...), custom_call_target="tpu_custom_call" | custom-call | flops 1073741824 | bytes 8388608 | tf_op jit(solution)/shard_map/pallas_call | solution.py:100
  80.7 6.9 %all-to-all-start = ((bf16[16,256,128]{2,1,0:T(8,128)(2,1)}), bf16[16,256,128]{2,1,0:T(8,128)(2,1)}, u32[]{:S(2)}, u32[]{:S(2)}) async-start(bf16[16,256,128]{2,1,0:T(8,128)(2,1)} %bitcast.136), calls=%async_computation | async-start | bytes 2097152 | tf_op jit(solution)/shard_map/all_to_all | solution.py:793
  97.0 16.0 %collective-permute-done.21 = bf16[128,2304]{1,0:T(8,128)(2,1)S(1)} collective-permute-done((bf16[128,2304]{1,0:T(8,128)(2,1)}, bf16[128,2304]{1,0:T(8,128)(2,1)S(1)}, u32[]{:S(2)}, u32[]{:S(2)}) %collective-permute-start.21) | collective-permute-done | bytes 589856 | tf_op jit(solution)/shard_map/ppermute | solution.py:717
  115.5 15.8 %collective-permute-done.17 = bf16[128,2304]{1,0:T(8,128)(2,1)} collective-permute-done((bf16[128,2304]{1,0:T(8,128)(2,1)}, bf16[128,2304]{1,0:T(8,128)(2,1)}, u32[]{:S(2)}, u32[]{:S(2)}) %collective-permute-start.17) | collective-permute-done | bytes 589856 | tf_op jit(solution)/shard_map/ppermute | solution.py:717
  138.3 7.6 %fusion.51.wo_ref = bf16[1024,1024]{1,0:T(8,128)(2,1)} fusion(bf16[1024,512]{1,0:T(8,128)(2,1)} %collective-permute-done.9, bf16[256,256]{1,0:T(8,128)(2,1)S(1)} %copy-done.53, bf16[256,256]{1,0:T(8,128)(2,1)S(1)} %copy-done.49, bf16[256,256]{1,0:T(8,128)(2,1)S(1)} %copy-done.51, bf16[256,256]{1,0:T(8,128)(2,1)S(1)} %copy-done.32, ...), kind=kOutput, calls=%fused_computation.62 | convolution fusion | flops 4329570304 | bytes 4202497 | tf_op jit(solution)/shard_map/dot_general | solution.py:32
  149.9 11.0 %collective-permute-done.18 = bf16[256,2304]{1,0:T(8,128)(2,1)} collective-permute-done((bf16[256,2304]{1,0:T(8,128)(2,1)}, bf16[256,2304]{1,0:T(8,128)(2,1)}, u32[]{:S(2)}, u32[]{:S(2)}) %collective-permute-start.18) | collective-permute-done | bytes 1179680 | tf_op jit(solution)/shard_map/ppermute | solution.py:717
  165.2 20.3 %shard_map.248 = (bf16[2048,128]{1,0:T(8,128)(2,1)}, f32[64,4096]{1,0:T(8,128)}, f32[1,4096]{1,0:T(1,128)}) custom-call(s32[1]{0:T(128)} %bitcast.core_ref, s32[32]{0:T(128)} %get-tuple-element.139.kslot_ref, s32[32]{0:T(128)} %get-tuple-element.138.qslot_ref, s32[4,8]{1,0:T(4,128)} %pad_add_fusion.lims_ref, bf16[4096,128]{1,0:T(8,128)(2,1)} %bitcast.31.q_ref.own_ref, ...), custom_call_target="tpu_custom_call" | custom-call | flops 8589934592 | bytes 8388608 | tf_op jit(solution)/shard_map/pallas_call | solution.py:249
  195.4 46.9 %all-to-all-done.1 = bf16[16,128,128]{2,1,0:T(8,128)(2,1)S(1)} async-done(((bf16[16,128,128]{2,1,0:T(8,128)(2,1)}), bf16[16,128,128]{2,1,0:T(8,128)(2,1)S(1)}, u32[]{:S(2)}, u32[]{:S(2)}) %all-to-all-start.1) | async-done | bytes 524320 | tf_op jit(solution)/shard_map/all_to_all | solution.py:793
  252.9 13.5 %shard_map.250 = (bf16[512,2304]{1,0:T(8,128)(2,1)}, bf16[512,2304]{1,0:T(8,128)(2,1)}, f32[512,1024]{1,0:T(8,128)}, f32[512,1024]{1,0:T(8,128)}) custom-call(bf16[512,1024]{1,0:T(8,128)(2,1)} %get-tuple-element.78.n_ref, bf16[1024,512]{1,0:T(8,128)(2,1)} %get-tuple-element.79.nt_ref, bf16[512,1024]{1,0:T(8,128)(2,1)} %copy-done.15, ...), custom_call_target="tpu_custom_call" | custom-call | flops 7247757312 | bytes 16777216 | tf_op jit(solution)/shard_map/pallas_call | solution.py:450
  266.4 14.7 %shard_map.251 = (bf16[512,2304]{1,0:T(8,128)(2,1)}, bf16[512,2304]{1,0:T(8,128)(2,1)}, f32[512,1024]{1,0:T(8,128)}, f32[512,1024]{1,0:T(8,128)}) custom-call(bf16[512,1024]{1,0:T(8,128)(2,1)} %get-tuple-element.78.n_ref, bf16[1024,512]{1,0:T(8,128)(2,1)} %get-tuple-element.79.nt_ref, bf16[512,1024]{1,0:T(8,128)(2,1)} %copy-done.15, ...), custom_call_target="tpu_custom_call" | custom-call | flops 7247757312 | bytes 16777216 | tf_op jit(solution)/shard_map/pallas_call | solution.py:450
  281.2 15.4 %shard_map.252 = (bf16[512,2304]{1,0:T(8,128)(2,1)}, bf16[512,2304]{1,0:T(8,128)(2,1)}, f32[512,1024]{1,0:T(8,128)}, bf16[512,1024]{1,0:T(8,128)(2,1)}) custom-call(bf16[512,1024]{1,0:T(8,128)(2,1)} %get-tuple-element.78.n_ref, bf16[1024,512]{1,0:T(8,128)(2,1)} %get-tuple-element.79.nt_ref, bf16[512,1024]{1,0:T(8,128)(2,1)} %copy-done.15, ...), custom_call_target="tpu_custom_call" | custom-call | flops 7247757312 | bytes 16777216 | tf_op jit(solution)/shard_map/pallas_call | solution.py:450
  307.0 6.2 %shard_map.253 = (f32[512,1024]{1,0:T(8,128)}, bf16[512,1024]{1,0:T(8,128)(2,1)}, f32[1,1024]{1,0:T(1,128)}, bf16[2048,128]{1,0:T(8,128)(2,1)}) custom-call(bf16[512,1024]{1,0:T(8,128)(2,1)} %get-tuple-element.91.back_ref, bf16[512,1024]{1,0:T(8,128)(2,1)} %collective-permute-done.25.other_ref, f32[512,1024]{1,0:T(8,128)} %get-tuple-element.77.res_ref, ...), custom_call_target="tpu_custom_call" | custom-call | flops 536870912 | bytes 10485760 | tf_op jit(solution)/shard_map/pallas_call | solution.py:636
  328.3 39.8 %all-to-all-done.2 = bf16[16,128,128]{2,1,0:T(8,128)(2,1)} async-done(((bf16[16,128,128]{2,1,0:T(8,128)(2,1)}), bf16[16,128,128]{2,1,0:T(8,128)(2,1)}, u32[]{:S(2)}, u32[]{:S(2)}) %all-to-all-start.2) | async-done | bytes 524320 | tf_op jit(solution)/shard_map/all_to_all | solution.py:793
  368.1 32.0 %shard_map.254 = (f32[4096,128]{1,0:T(8,128)}, f32[4096,128]{1,0:T(8,128)}, bf16[4096,128]{1,0:T(8,128)(2,1)}) custom-call(s32[1]{0:T(128)} %bitcast.core_ref, s32[32]{0:T(128)} %get-tuple-element.139.kslot_ref, s32[32]{0:T(128)} %get-tuple-element.138.qslot_ref, s32[4,8]{1,0:T(4,128)} %pad_add_fusion.lims_ref, bf16[4096,128]{1,0:T(8,128)(2,1)} %bitcast.31.q_ref.own_ref, ...), custom_call_target="tpu_custom_call" | custom-call | flops 17179869184 | bytes 8388608 | tf_op jit(solution)/shard_map/pallas_call | solution.py:359
  429.5 6.4 %all-to-all-done.3 = bf16[16,256,128]{2,1,0:T(8,128)(2,1)S(1)} async-done(((bf16[16,256,128]{2,1,0:T(8,128)(2,1)}), bf16[16,256,128]{2,1,0:T(8,128)(2,1)S(1)}, u32[]{:S(2)}, u32[]{:S(2)}) %all-to-all-start.3) | async-done | bytes 1048608 | tf_op jit(solution)/shard_map/all_to_all | solution.py:793
  436.9 8.1 %shard_map.255 = (bf16[512,1024]{1,0:T(8,128)(2,1)}, f32[8,8,128]{2,1,0:T(8,128)}) custom-call(s32[1]{0:T(128)} %bitcast.core_ref, bf16[8,2,256,128]{3,2,1,0:T(8,128)(2,1)} %bitcast.133, f32[512,1024]{1,0:T(8,128)} %get-tuple-element.99.raw_ref, f32[1,128]{1,0:T(1,128)} %maximum_bitcast_fusion.gain_ref, f32[256,128]{1,0:T(8,128)} %get-tuple-element.197.cos_ref, ...), custom_call_target="tpu_custom_call" | custom-call | flops 16777216 | bytes 8388608 | tf_op jit(solution)/shard_map/pallas_call | solution.py:139
  457.2 18.3 %collective-permute-done.30 = bf16[512,768]{1,0:T(8,128)(2,1)S(1)} collective-permute-done((bf16[512,768]{1,0:T(8,128)(2,1)S(1)}, bf16[512,768]{1,0:T(8,128)(2,1)S(1)}, u32[]{:S(2)}, u32[]{:S(2)}) %collective-permute-start.30) | collective-permute-done | bytes 786464 | tf_op jit(solution)/shard_map/ppermute | solution.py:717
  475.6 19.3 %collective-permute-done.28 = bf16[512,768]{1,0:T(8,128)(2,1)S(1)} collective-permute-done((bf16[512,768]{1,0:T(8,128)(2,1)S(1)}, bf16[512,768]{1,0:T(8,128)(2,1)S(1)}, u32[]{:S(2)}, u32[]{:S(2)}) %collective-permute-start.28) | collective-permute-done | bytes 786464 | tf_op jit(solution)/shard_map/ppermute | solution.py:717
  549.7 15.6 %collective-permute-done.37 = bf16[128,2304]{1,0:T(8,128)(2,1)} collective-permute-done((bf16[128,2304]{1,0:T(8,128)(2,1)}, bf16[128,2304]{1,0:T(8,128)(2,1)}, u32[]{:S(2)}, u32[]{:S(2)}) %collective-permute-start.37) | collective-permute-done | bytes 589856 | tf_op jit(solution)/shard_map/ppermute | solution.py:717
  566.4 7.3 %collective-permute-done.32 = bf16[128,1536]{1,0:T(8,128)(2,1)S(1)} collective-permute-done((bf16[128,1536]{1,0:T(8,128)(2,1)S(1)}, bf16[128,1536]{1,0:T(8,128)(2,1)S(1)}, u32[]{:S(2)}, u32[]{:S(2)}) %collective-permute-start.32) | collective-permute-done | bytes 393248 | tf_op jit(solution)/shard_map/ppermute | solution.py:717
  576.2 16.1 %collective-permute-done.38 = bf16[64,2304]{1,0:T(8,128)(2,1)S(1)} collective-permute-done((bf16[64,2304]{1,0:T(8,128)(2,1)S(1)}, bf16[64,2304]{1,0:T(8,128)(2,1)S(1)}, u32[]{:S(2)}, u32[]{:S(2)}) %collective-permute-start.38) | collective-permute-done | bytes 294944 | tf_op jit(solution)/shard_map/ppermute | solution.py:717
  (443 shorter events, 230.4 us)
Async XLA Ops:
  4.3 40.9 %collective-permute-start.11 = (bf16[32,6912]{1,0:T(8,128)(2,1)}, bf16[32,6912]{1,0:T(8,128)(2,1)}, u32[]{:S(2)}, u32[]{:S(2)}) collective-permute-start(bf16[32,6912]{1,0:T(8,128)(2,1)} %get-tuple-element.81), channel_id=1, source_target_pairs={{0,1},{1,0},{2,3},{3,2},{4,5},{5,4},{6,7},{7,6},{8,9},{9,8},{10,11... | collective-permute-start | bytes 1327112 | tf_op jit(solution)/shard_map/ppermute | solution.py:723
  50.0 40.9 %collective-permute-start.16 = (bf16[64,2304]{1,0:T(8,128)(2,1)S(1)}, bf16[64,2304]{1,0:T(8,128)(2,1)S(1)}, u32[]{:S(2)}, u32[]{:S(2)}) collective-permute-start(bf16[64,2304]{1,0:T(8,128)(2,1)S(1)} %maximum_select_fusion.13), channel_id=1, source_target_pairs={{0,16},{2,18},{4,20},{6,22},{8,24},{10,26},{12,28},{14,30},{16,0},... | collective-permute-start | bytes 884744 | tf_op jit(solution)/shard_map/ppermute | solution.py:717
  50.1 43.4 %collective-permute-start.12 = (bf16[64,2304]{1,0:T(8,128)(2,1)S(1)}, bf16[64,2304]{1,0:T(8,128)(2,1)S(1)}, u32[]{:S(2)}, u32[]{:S(2)}) collective-permute-start(bf16[64,2304]{1,0:T(8,128)(2,1)S(1)} %maximum_select_fusion.12), channel_id=1, source_target_pairs={{0,16},{2,18},{4,20},{6,22},{8,24},{10,26},{12,28},{14,30},{16,0},... | collective-permute-start | bytes 884744 | tf_op jit(solution)/shard_map/ppermute | solution.py:717
  79.0 59.2 %collective-permute-start.9 = (bf16[1024,512]{1,0:T(8,128)(2,1)}, bf16[1024,512]{1,0:T(8,128)(2,1)}, u32[]{:S(2)}, u32[]{:S(2)}) collective-permute-start(bf16[1024,512]{1,0:T(8,128)(2,1)} %maximum_maximum_fusion), channel_id=1, source_target_pairs={{0,1},{1,0},{2,3},{3,2},{4,5},{5,4},{6,7},{7,6},{8,9},{9,8},{10,11... | collective-permute-start | bytes 3145736 | tf_op jit(solution)/shard_map/ppermute | solution.py:723
  80.7 56.4 %all-to-all-start = ((bf16[16,256,128]{2,1,0:T(8,128)(2,1)}), bf16[16,256,128]{2,1,0:T(8,128)(2,1)}, u32[]{:S(2)}, u32[]{:S(2)}) async-start(bf16[16,256,128]{2,1,0:T(8,128)(2,1)} %bitcast.136), calls=%async_computation | async-start | bytes 2097152 | tf_op jit(solution)/shard_map/all_to_all | solution.py:793
  94.4 40.3 %collective-permute-start.13 = (bf16[128,2304]{1,0:T(8,128)(2,1)}, bf16[128,2304]{1,0:T(8,128)(2,1)}, u32[]{:S(2)}, u32[]{:S(2)}) collective-permute-start(bf16[128,2304]{1,0:T(8,128)(2,1)} %pad_maximum_fusion.11), channel_id=1, source_target_pairs={{0,2},{2,0},{4,6},{6,4},{8,10},{10,8},{12,14},{14,12},{16,18},{18,... | collective-permute-start | bytes 1769480 | tf_op jit(solution)/shard_map/ppermute | solution.py:717
  136.9 54.0 %collective-permute-start.14 = (bf16[256,2304]{1,0:T(8,128)(2,1)}, bf16[256,2304]{1,0:T(8,128)(2,1)}, u32[]{:S(2)}, u32[]{:S(2)}) collective-permute-start(bf16[256,2304]{1,0:T(8,128)(2,1)} %pad_maximum_fusion.3), channel_id=1, source_target_pairs={{0,4},{2,6},{4,0},{6,2},{8,12},{10,14},{12,8},{14,10},{16,20},{18,... | collective-permute-start | bytes 3538952 | tf_op jit(solution)/shard_map/ppermute | solution.py:717
  148.7 104.2 %collective-permute-start.23 = (bf16[512,2304]{1,0:T(8,128)(2,1)}, bf16[512,2304]{1,0:T(8,128)(2,1)}, u32[]{:S(2)}, u32[]{:S(2)}) collective-permute-start(bf16[512,2304]{1,0:T(8,128)(2,1)} %pad_maximum_fusion.2.refs_0_), channel_id=1, source_target_pairs={{0,4},{2,6},{4,0},{6,2},{8,12},{10,14},{12,8},{14,10},{16,20},{18,... | collective-permute-start | bytes 7077896 | tf_op jit(solution)/shard_map/ppermute | solution.py:717
  163.9 102.5 %collective-permute-start.19 = (bf16[512,2304]{1,0:T(8,128)(2,1)}, bf16[512,2304]{1,0:T(8,128)(2,1)}, u32[]{:S(2)}, u32[]{:S(2)}) collective-permute-start(bf16[512,2304]{1,0:T(8,128)(2,1)} %pad_maximum_fusion.1.refs_0_), channel_id=1, source_target_pairs={{0,2},{2,0},{4,6},{6,4},{8,10},{10,8},{12,14},{14,12},{16,18},{18,... | collective-permute-start | bytes 7077896 | tf_op jit(solution)/shard_map/ppermute | solution.py:717
  185.5 56.9 %all-to-all-start.1 = ((bf16[16,128,128]{2,1,0:T(8,128)(2,1)}), bf16[16,128,128]{2,1,0:T(8,128)(2,1)S(1)}, u32[]{:S(2)}, u32[]{:S(2)}) async-start(bf16[16,128,128]{2,1,0:T(8,128)(2,1)} %bitcast.138), calls=%async_computation.1 | async-start | bytes 1048576 | tf_op jit(solution)/shard_map/all_to_all | solution.py:793
  193.9 87.2 %collective-permute-start.15 = (bf16[512,2304]{1,0:T(8,128)(2,1)}, bf16[512,2304]{1,0:T(8,128)(2,1)}, u32[]{:S(2)}, u32[]{:S(2)}) collective-permute-start(bf16[512,2304]{1,0:T(8,128)(2,1)} %pad_maximum_fusion.refs_0_), channel_id=1, source_target_pairs={{0,8},{2,10},{4,12},{6,14},{8,0},{10,2},{12,4},{14,6},{16,24},{18,... | collective-permute-start | bytes 7077896 | tf_op jit(solution)/shard_map/ppermute | solution.py:717
  304.5 103.5 %collective-permute-start.43 = (bf16[512,2304]{1,0:T(8,128)(2,1)}, bf16[512,2304]{1,0:T(8,128)(2,1)S(1)}, u32[]{:S(2)}, u32[]{:S(2)}) collective-permute-start(bf16[512,2304]{1,0:T(8,128)(2,1)} %get-tuple-element.121), channel_id=1, source_target_pairs={{0,8},{2,10},{4,12},{6,14},{8,0},{10,2},{12,4},{14,6},{16,24},{18,... | collective-permute-start | bytes 7077896 | tf_op jit(solution)/shard_map/ppermute | solution.py:717
  304.6 115.4 %collective-permute-start.39 = (bf16[512,2304]{1,0:T(8,128)(2,1)}, bf16[512,2304]{1,0:T(8,128)(2,1)}, u32[]{:S(2)}, u32[]{:S(2)}) collective-permute-start(bf16[512,2304]{1,0:T(8,128)(2,1)} %get-tuple-element.116), channel_id=1, source_target_pairs={{0,2},{2,0},{4,6},{6,4},{8,10},{10,8},{12,14},{14,12},{16,18},{18,... | collective-permute-start | bytes 7077896 | tf_op jit(solution)/shard_map/ppermute | solution.py:717
  305.8 118.4 %collective-permute-start.35 = (bf16[512,2304]{1,0:T(8,128)(2,1)}, bf16[512,2304]{1,0:T(8,128)(2,1)}, u32[]{:S(2)}, u32[]{:S(2)}) collective-permute-start(bf16[512,2304]{1,0:T(8,128)(2,1)} %get-tuple-element.110), channel_id=1, source_target_pairs={{0,4},{2,6},{4,0},{6,2},{8,12},{10,14},{12,8},{14,10},{16,20},{18,... | collective-permute-start | bytes 7077896 | tf_op jit(solution)/shard_map/ppermute | solution.py:717
  313.2 54.8 %all-to-all-start.2 = ((bf16[16,128,128]{2,1,0:T(8,128)(2,1)}), bf16[16,128,128]{2,1,0:T(8,128)(2,1)}, u32[]{:S(2)}, u32[]{:S(2)}) async-start(bf16[16,128,128]{2,1,0:T(8,128)(2,1)} %bitcast.137), calls=%async_computation.2 | async-start | bytes 1048576 | tf_op jit(solution)/shard_map/all_to_all | solution.py:793
  320.8 83.9 %collective-permute-start.24 = (f32[256,1024]{1,0:T(8,128)}, f32[256,1024]{1,0:T(8,128)}, u32[]{:S(2)}, u32[]{:S(2)}) collective-permute-start(f32[256,1024]{1,0:T(8,128)} %slice_select_fusion.4), channel_id=1, source_target_pairs={{0,1},{1,0},{2,3},{3,2},{4,5},{5,4},{6,7},{7,6},{8,9},{9,8},{10,11... | collective-permute-start | bytes 3145736 | tf_op jit(solution)/shard_map/ppermute | solution.py:723
  424.1 78.1 %collective-permute-start.40 = (bf16[256,2304]{1,0:T(8,128)(2,1)}, bf16[256,2304]{1,0:T(8,128)(2,1)}, u32[]{:S(2)}, u32[]{:S(2)}) collective-permute-start(bf16[256,2304]{1,0:T(8,128)(2,1)} %get-tuple-element.145), channel_id=1, source_target_pairs={{0,4},{2,6},{4,0},{6,2},{8,12},{10,14},{12,8},{14,10},{16,20},{18,... | collective-permute-start | bytes 3538952 | tf_op jit(solution)/shard_map/ppermute | solution.py:717
  428.0 77.1 %collective-permute-start.36 = (bf16[256,2304]{1,0:T(8,128)(2,1)}, bf16[256,2304]{1,0:T(8,128)(2,1)}, u32[]{:S(2)}, u32[]{:S(2)}) collective-permute-start(bf16[256,2304]{1,0:T(8,128)(2,1)} %get-tuple-element.147), channel_id=1, source_target_pairs={{0,2},{2,0},{4,6},{6,4},{8,10},{10,8},{12,14},{14,12},{16,18},{18,... | collective-permute-start | bytes 3538952 | tf_op jit(solution)/shard_map/ppermute | solution.py:717
  449.2 45.7 %collective-permute-start.28 = (bf16[512,768]{1,0:T(8,128)(2,1)S(1)}, bf16[512,768]{1,0:T(8,128)(2,1)S(1)}, u32[]{:S(2)}, u32[]{:S(2)}) collective-permute-start(bf16[512,768]{1,0:T(8,128)(2,1)S(1)} %fusion.109), channel_id=1, source_target_pairs={{0,4},{2,6},{4,0},{6,2},{8,12},{10,14},{12,8},{14,10},{16,20},{18,... | collective-permute-start | bytes 2359304 | tf_op jit(solution)/shard_map/ppermute | solution.py:717
  455.0 51.4 %collective-permute-start.27 = (f32[256,1024]{1,0:T(8,128)S(1)}, f32[256,1024]{1,0:T(8,128)S(1)}, u32[]{:S(2)}, u32[]{:S(2)}) collective-permute-start(f32[256,1024]{1,0:T(8,128)S(1)} %slice_select_fusion.3), channel_id=1, source_target_pairs={{0,1},{1,0},{2,3},{3,2},{4,5},{5,4},{6,7},{7,6},{8,9},{9,8},{10,11... | collective-permute-start | bytes 3145736 | tf_op jit(solution)/shard_map/ppermute | solution.py:723
  497.9 47.1 %collective-permute-start.45 = (bf16[128,2304]{1,0:T(8,128)(2,1)}, bf16[128,2304]{1,0:T(8,128)(2,1)}, u32[]{:S(2)}, u32[]{:S(2)}) collective-permute-start(bf16[128,2304]{1,0:T(8,128)(2,1)} %get-tuple-element.149), channel_id=1, source_target_pairs={{0,2},{2,0},{4,6},{6,4},{8,10},{10,8},{12,14},{14,12},{16,18},{18,... | collective-permute-start | bytes 1769480 | tf_op jit(solution)/shard_map/ppermute | solution.py:717
  499.9 42.5 %collective-permute-start.31 = (bf16[256,768]{1,0:T(8,128)(2,1)}, bf16[256,768]{1,0:T(8,128)(2,1)S(1)}, u32[]{:S(2)}, u32[]{:S(2)}) collective-permute-start(bf16[256,768]{1,0:T(8,128)(2,1)} %add_convert_fusion.5), channel_id=1, source_target_pairs={{0,4},{2,6},{4,0},{6,2},{8,12},{10,14},{12,8},{14,10},{16,20},{18,... | collective-permute-start | bytes 1179656 | tf_op jit(solution)/shard_map/ppermute | solution.py:717
  502.2 41.4 %collective-permute-start.29 = (bf16[256,768]{1,0:T(8,128)(2,1)}, bf16[256,768]{1,0:T(8,128)(2,1)}, u32[]{:S(2)}, u32[]{:S(2)}) collective-permute-start(bf16[256,768]{1,0:T(8,128)(2,1)} %add_convert_fusion.6), channel_id=1, source_target_pairs={{0,2},{2,0},{4,6},{6,4},{8,10},{10,8},{12,14},{14,12},{16,18},{18,... | collective-permute-start | bytes 1179656 | tf_op jit(solution)/shard_map/ppermute | solution.py:717
  505.2 42.9 %collective-permute-start.41 = (bf16[128,2304]{1,0:T(8,128)(2,1)}, bf16[128,2304]{1,0:T(8,128)(2,1)}, u32[]{:S(2)}, u32[]{:S(2)}) collective-permute-start(bf16[128,2304]{1,0:T(8,128)(2,1)} %get-tuple-element.151), channel_id=1, source_target_pairs={{0,8},{2,10},{4,12},{6,14},{8,0},{10,2},{12,4},{14,6},{16,24},{18,... | collective-permute-start | bytes 1769480 | tf_op jit(solution)/shard_map/ppermute | solution.py:717
  (125 other events, 2008.8 us)
